TPU v7x, 32 devices: a whole 2x2x4 slice. The times are simulated.
32 devices in a mesh: depth: 4 (over y, x), rows: 8 (over z, core).
Axes of the slice: x: 2, y: 2, z: 4, core: 2. Of those that a mesh axis runs over, the one named last changes fastest.
Arguments:
- tokens: bfloat16 [16, 1024, 1152], P('depth', 'rows'), may hold values from -6 to 6
- cotangent: bfloat16 [16, 1024, 1152], P('depth', 'rows'), may hold values from -6 to 6
- exit_depth: int32 [16, 1024], P('depth', 'rows'), may hold values from 0 to 3
- lengths: int32 [16], replicated, may hold values from 256 to 1024, as said below
- loop_index: int32 [16], replicated, may hold values from 0 to 3, as said below
- attn_gain: bfloat16 [1152], P(('depth', 'rows')), may hold values from 0.099609375 to 1.8984375
- mlp_gain: bfloat16 [1152], P(('depth', 'rows')), may hold values from 0.099609375 to 1.8984375
- qkv_weight: bfloat16 [1152, 1536], P(('depth', 'rows')), may hold values from -0.1875 to 0.1875
- out_weight: bfloat16 [1024, 1152], P(('depth', 'rows')), may hold values from -0.5 to 0.5
- gateup_weight: bfloat16 [1152, 13824], P(('depth', 'rows')), may hold values from -0.1875 to 0.1875
- down_weight: bfloat16 [6912, 1152], P(('depth', 'rows')), may hold values from -0.078125 to 0.078125
- qkv_enter: bfloat16 [4, 1152, 768], P('depth', 'rows'), may hold values from -0.1875 to 0.1875
- query_leave: bfloat16 [4, 256, 1024], P('depth', 'rows'), may hold values from -0.375 to 0.375
- kv_leave: bfloat16 [4, 256, 512], P('depth', 'rows'), may hold values from -0.375 to 0.375
- out_enter: bfloat16 [4, 1024, 256], P('depth', 'rows'), may hold values from -0.5 to 0.5
- out_leave: bfloat16 [4, 256, 1152], P('depth', 'rows'), may hold values from -0.375 to 0.375
- gateup_enter: bfloat16 [4, 1152, 512], P('depth', 'rows'), may hold values from -0.1875 to 0.1875
- gateup_leave: bfloat16 [4, 256, 13824], P('depth', 'rows'), may hold values from -0.375 to 0.375
- down_enter: bfloat16 [4, 6912, 256], P('depth', 'rows'), may hold values from -0.078125 to 0.078125
- down_leave: bfloat16 [4, 256, 1152], P('depth', 'rows'), may hold values from -0.375 to 0.375
Outputs:
- activations: bfloat16 [16, 1024, 1152], P('depth', 'rows')
- grad_tokens: bfloat16 [16, 1024, 1152], P('depth', 'rows')
- exit_counts: int32 [4], replicated
- confidence: float32 [], replicated
- grad_attn_gain: float32 [1152], P(('depth', 'rows'))
- grad_mlp_gain: float32 [1152], P(('depth', 'rows'))
- grad_qkv_weight: float32 [1152, 1536], P(('depth', 'rows'))
- grad_out_weight: float32 [1024, 1152], P(('depth', 'rows'))
- grad_gateup_weight: float32 [1152, 13824], P(('depth', 'rows'))
- grad_down_weight: float32 [6912, 1152], P(('depth', 'rows'))
- grad_qkv_enter: float32 [4, 1152, 768], P('depth', 'rows')
- grad_query_leave: float32 [4, 256, 1024], P('depth', 'rows')
- grad_kv_leave: float32 [4, 256, 512], P('depth', 'rows')
- grad_out_enter: float32 [4, 1024, 256], P('depth', 'rows')
- grad_out_leave: float32 [4, 256, 1152], P('depth', 'rows')
- grad_gateup_enter: float32 [4, 1152, 512], P('depth', 'rows')
- grad_gateup_leave: float32 [4, 256, 13824], P('depth', 'rows')
- grad_down_enter: float32 [4, 6912, 256], P('depth', 'rows')
- grad_down_leave: float32 [4, 256, 1152], P('depth', 'rows')
Inputs may be any that keep to these rules, and one draw needn't show every extreme that they name: `loop_index`: each aligned block of 4 entries is a permutation of the loops 0 to 3. `lengths`: for every loop, at least one of the sequence slots with that loop index has length 1024.
All inputs are finite; a program needn't handle non-finite values.
Results may differ from a plain program's by a relative error of at most 0.028.
Values may be sent and summed in bfloat16 or wider, within the bound.
No kernel may reach another device: no remote copies, remote signals or barrier semaphores. Data moves between devices by JAX's collectives and lax.ppermute only.
A program may use at most 240 MiB of HBM per device.

v0:
```python
import math

import jax
import jax.numpy as jnp
from jax import lax
from jax.experimental import pallas as pl
from jax.experimental.pallas import tpu as pltpu
from jax.sharding import PartitionSpec as P

BF = jnp.bfloat16
F32 = jnp.float32
ROOT = math.sqrt(2.0 / math.pi)
CUBE = 0.044715


def angles(positions, size):
    freqs = jnp.exp(jnp.arange(size // 2, dtype=F32) * (-2.0 * math.log(10000.0) / size))
    phase = positions[:, None] * freqs[None, :]
    return (jnp.cos(phase), jnp.sin(phase))


def matmul(left, right):
    return jnp.dot(left, right, preferred_element_type=F32)


def outer_sum(left, right):
    return lax.dot_general(left, right, (((0,), (0,)), ((), ())), preferred_element_type=F32)


def through(left, right):
    return lax.dot_general(left, right, (((1,), (1,)), ((), ())), preferred_element_type=F32)


def swap(value, axis, flip):
    size = lax.axis_size(axis)
    return lax.ppermute(value, axis, [(i, i ^ flip) for i in range(size)])


def add_low(left, right):
    return (left.astype(F32) + right.astype(F32)).astype(BF)


def tie(*values):
    return lax.optimization_barrier(values)


def bits_of(size):
    return [1 << i for i in range(size.bit_length() - 1)]


LANES = 256


def even(height):
    return -(-height // 16) * 16


def segments(shapes):
    out, row = [], 0
    for which, (height, columns) in enumerate(shapes):
        for start in range(0, columns, LANES):
            out.append((which, row, start, min(LANES, columns - start)))
            row += even(height)
    return out, row


def put(out_ref, lead, row, height, value):
    short, narrow = even(height) - height, LANES - value.shape[1]
    if narrow:
        value = jnp.concatenate([value, jnp.zeros((height, narrow), value.dtype)], axis=1)
    if short:
        value = jnp.concatenate([value, jnp.zeros((short, LANES), value.dtype)], axis=0)
    out_ref[lead, row : row + even(height), :] = value


def pack_kernel(shapes, *refs):
    where, _ = segments(shapes)
    for which, row, start, size in where:
        put(refs[-1], 0, row, shapes[which][0], refs[which][:, start : start + size])


def pack_pass(arrays):
    shapes = [array.shape for array in arrays]
    return pl.pallas_call(
        lambda *refs: pack_kernel(shapes, *refs),
        out_shape=jax.ShapeDtypeStruct((1, segments(shapes)[1], LANES), BF),
        compiler_params=MEMORY,
        cost_estimate=FREE,
    )(*arrays)


def unpack_kernel(shapes, into, in_ref, *outs):
    for which, row, start, size in segments(shapes)[0]:
        height = shapes[which][0]
        out, column = into[which]
        column += start
        for lead in range(in_ref.shape[0]):
            value = in_ref[lead, row : row + height, :size]
            first = lead * height
            outs[out][first : first + height, column : column + size] = value.astype(
                outs[out].dtype
            )


def unpack_pass(packed, shapes, dtype, groups=None):
    lead = packed.shape[0]
    groups = groups or [[which] for which in range(len(shapes))]
    into, out_shapes = {}, []
    for out, group in enumerate(groups):
        column = 0
        for which in group:
            into[which] = (out, column)
            column += shapes[which][1]
        shape = (lead * shapes[group[0]][0], column)
        out_shapes.append(jax.ShapeDtypeStruct(shape, dtype))
    return pl.pallas_call(
        lambda *refs: unpack_kernel(shapes, into, *refs),
        out_shape=out_shapes,
        compiler_params=MEMORY,
        cost_estimate=FREE,
    )(packed)


def spread_rows(pos_ref, out_ref, row, value, first, size):
    leads = out_ref.shape[0]
    height = value.shape[0] // leads
    for lead in range(leads):
        block = value[lead * height : (lead + 1) * height, first : first + size]
        put(out_ref, pos_ref[lead], row, height, block.astype(BF))


def total_of(refs, rows, columns):
    total = refs[0][rows, :columns].astype(F32)
    for ref in refs[1:]:
        total = total + ref[rows, :columns].astype(F32)
    return total


def place_all(pos_ref, out_ref, values):
    shapes = [(value.shape[0] // out_ref.shape[0], value.shape[1]) for value in values]
    for which, row, start, size in segments(shapes)[0]:
        spread_rows(pos_ref, out_ref, row, values[which], start, size)


def attn_grads_kernel(height, bands, pos_ref, *refs):
    grad_ref, enter_ref, leave_ref, out_ref = refs[-4:]
    rank = leave_ref.shape[0]
    values = [total_of(refs[:-4], slice(0, height), grad_ref.shape[1])]
    for start, size in bands:
        values.append(through(grad_ref[:, start : start + size], leave_ref[:, start : start + size]))
    for index, (start, size) in enumerate(bands):
        enter = enter_ref[:, index * rank : (index + 1) * rank]
        values.append(outer_sum(enter, grad_ref[:, start : start + size]))
    place_all(pos_ref, out_ref, values)


def attn_grads_shapes(rows, height, grad, enter, leave, bands):
    rank = leave.shape[0]
    return (
        [(height // rows, grad.shape[1])]
        + [(grad.shape[0] // rows, rank)] * len(bands)
        + [(rank // rows, size) for _, size in bands]
    )


def rest_grads_kernel(first, pos_ref, *refs):
    (
        grad_out_ref,
        out_enter_ref,
        out_leave_ref,
        grad_gateup_ref,
        leave_ref,
        grad_down_ref,
        down_enter_ref,
        out_ref,
    ) = refs[-8:]
    shard = leave_ref.shape[1] // 2
    values = [
        total_of(refs[:-8], slice(first, refs[0].shape[0]), grad_out_ref.shape[1]),
        through(grad_out_ref[...], out_leave_ref[...]),
        outer_sum(out_enter_ref[...], grad_out_ref[...]),
        through(grad_gateup_ref[:, :shard], leave_ref[:, :shard]),
        through(grad_gateup_ref[:, shard:], leave_ref[:, shard:]),
        outer_sum(down_enter_ref[...], grad_down_ref[...]),
    ]
    place_all(pos_ref, out_ref, values)


def grads_pass(kernel, pos, rows, shapes, arrays):
    whole = [pl.BlockSpec(memory_space=pltpu.VMEM)] * len(arrays)
    shape = (rows, segments(shapes)[1], LANES)
    return pl.pallas_call(
        kernel,
        in_specs=[pl.BlockSpec(memory_space=pltpu.SMEM)] + whole,
        out_specs=pl.BlockSpec(memory_space=pltpu.VMEM),
        out_shape=jax.ShapeDtypeStruct(shape, BF),
        compiler_params=MEMORY,
        cost_estimate=FREE,
    )(pos, *arrays)


FREE = pl.CostEstimate(flops=0, transcendentals=0, bytes_accessed=0)
MEMORY = pltpu.CompilerParams(vmem_limit_bytes=60 << 20)


def held(array):
    return pl.BlockSpec(
        array.shape, lambda *_: (0,) * len(array.shape), pipeline_mode=pl.Buffered(1)
    )


def strip(tile, columns):
    return pl.BlockSpec((tile, columns), lambda i: (i, 0))


def mean_scale(values):
    return lax.rsqrt(jnp.mean(values * values, axis=-1, keepdims=True) + 1e-06)


def turned(values, cosine, sine):
    half = values.shape[-1] // 2
    first, second = values[:, :half], values[:, half:]
    return jnp.concatenate(
        [first * cosine - second * sine, second * cosine + first * sine], axis=-1
    )


def enter_kernel(x_ref, gain_ref, weight_ref, cos_ref, sin_ref, n_ref, q_ref, kv_ref):
    head = kv_ref.shape[1] // 2
    width_q = q_ref.shape[1]
    values = x_ref[...].astype(F32)
    normed = (values * mean_scale(values) * gain_ref[...]).astype(BF)
    n_ref[...] = normed
    joined = matmul(normed, weight_ref[...])
    cosine, sine = cos_ref[...], sin_ref[...]
    scale = head ** (-0.5)
    for start in range(0, width_q, head):
        spun = turned(joined[:, start : start + head], cosine, sine)
        q_ref[:, start : start + head] = (spun * scale).astype(BF)
    kv_ref[:, :head] = turned(joined[:, width_q : width_q + head], cosine, sine).astype(BF)
    kv_ref[:, head:] = joined[:, width_q + head :].astype(BF)


def enter_pass(x, gain, weight, cosine, sine, width_q):
    count, width = x.shape
    tile = count // 2
    rest = weight.shape[1] - width_q
    return pl.pallas_call(
        enter_kernel,
        grid=(count // tile,),
        in_specs=[
            strip(tile, width),
            held(gain),
            held(weight),
            strip(tile, cosine.shape[1]),
            strip(tile, cosine.shape[1]),
        ],
        out_specs=[strip(tile, width), strip(tile, width_q), strip(tile, rest)],
        out_shape=[
            jax.ShapeDtypeStruct((count, width), BF),
            jax.ShapeDtypeStruct((count, width_q), BF),
            jax.ShapeDtypeStruct((count, rest), BF),
        ],
        compiler_params=MEMORY,
        cost_estimate=FREE,
    )(x, gain, weight, cosine, sine)


def stack_heads(ref, head):
    return jnp.concatenate(
        [ref[:, start : start + head] for start in range(0, ref.shape[1], head)], axis=0
    )


def allowed_keys(size_ref, pos_ref, key_ref, heads):
    fits = (key_ref[...] <= pos_ref[...]) & (key_ref[...] < size_ref[0])
    return jnp.concatenate([jnp.where(fits, 0.0, -1e30)] * heads, axis=0)


def attend_kernel(size_ref, q_ref, kv_ref, pos_ref, key_ref, o_ref, lse_ref):
    head = kv_ref.shape[1] // 2
    tile = q_ref.shape[0]
    heads = q_ref.shape[1] // head
    scores = through(stack_heads(q_ref, head), kv_ref[:, :head])
    scores = scores + allowed_keys(size_ref, pos_ref, key_ref, heads)
    highest = jnp.max(scores, axis=-1, keepdims=True)
    raised = jnp.exp(scores - highest)
    total = jnp.sum(raised, axis=-1, keepdims=True)
    probs = (raised * (1.0 / total)).astype(BF)
    lse_ref[...] = (highest + jnp.log(total)).reshape(1, heads * tile, 1)
    mixed = matmul(probs, kv_ref[:, head:]).astype(BF)
    for index in range(heads):
        o_ref[:, index * head : (index + 1) * head] = mixed[index * tile : (index + 1) * tile]


def attend_pass(size, q, kv, positions, key_positions, tile):
    count, width_q = q.shape
    heads = 2 * width_q // kv.shape[1]
    steps = count // tile

    def rows(columns):
        return pl.BlockSpec((tile, columns), lambda i, s: (i, 0))

    return pl.pallas_call(
        attend_kernel,
        grid_spec=pltpu.PrefetchScalarGridSpec(
            num_scalar_prefetch=1,
            grid=(steps,),
            in_specs=[rows(width_q), held(kv), rows(1), held(key_positions)],
            out_specs=[rows(width_q), pl.BlockSpec((1, heads * tile, 1), lambda i, s: (i, 0, 0))],
        ),
        out_shape=[
            jax.ShapeDtypeStruct((count, width_q), BF),
            jax.ShapeDtypeStruct((steps, heads * tile, 1), F32),
        ],
        compiler_params=MEMORY,
        cost_estimate=FREE,
    )(size, q, kv, positions, key_positions)


def attend_back_kernel(
    size_ref, q_ref, kv_ref, do_ref, lse_ref, pos_ref, key_ref, cos_ref, sin_ref, dq_ref, dkv_ref, acc
):
    head = kv_ref.shape[1] // 2
    tile = q_ref.shape[0]
    heads = q_ref.shape[1] // head
    step = pl.program_id(0)
    queries = stack_heads(q_ref, head)
    grads = stack_heads(do_ref, head)
    keys = kv_ref[:, :head]
    scores = through(queries, keys) + allowed_keys(size_ref, pos_ref, key_ref, heads)
    probs = jnp.exp(scores - lse_ref[0])
    grad_probs = through(grads, kv_ref[:, head:])
    centre = jnp.sum(probs * grad_probs, axis=-1, keepdims=True)
    grad_scores = (probs * (grad_probs - centre)).astype(BF)
    grad_q = matmul(grad_scores, keys) * (head ** (-0.5))
    cosine, sine = cos_ref[...], -sin_ref[...]
    for index in range(heads):
        spun = turned(grad_q[index * tile : (index + 1) * tile], cosine, sine)
        dq_ref[:, index * head : (index + 1) * head] = spun.astype(BF)
    grad_k = outer_sum(grad_scores, queries)
    grad_v = outer_sum(probs.astype(BF), grads)

    @pl.when(step == 0)
    def _():
        acc[:, :head] = grad_k
        acc[:, head:] = grad_v

    @pl.when(step > 0)
    def _():
        acc[:, :head] += grad_k
        acc[:, head:] += grad_v

    @pl.when(step == pl.num_programs(0) - 1)
    def _():
        dkv_ref[...] = acc[...].astype(BF)


def attend_back_pass(size, q, kv, do, lse, positions, key_positions, cosine, sine, tile):
    count, width_q = q.shape
    heads = 2 * width_q // kv.shape[1]

    def rows(columns):
        return pl.BlockSpec((tile, columns), lambda i, s: (i, 0))

    return pl.pallas_call(
        attend_back_kernel,
        grid_spec=pltpu.PrefetchScalarGridSpec(
            num_scalar_prefetch=1,
            grid=(count // tile,),
            in_specs=[
                rows(width_q),
                held(kv),
                rows(width_q),
                pl.BlockSpec((1, heads * tile, 1), lambda i, s: (i, 0, 0)),
                rows(1),
                held(key_positions),
                rows(cosine.shape[1]),
                rows(cosine.shape[1]),
            ],
            out_specs=[rows(width_q), pl.BlockSpec(kv.shape, lambda i, s: (0, 0))],
            scratch_shapes=[pltpu.VMEM(kv.shape, F32)],
        ),
        out_shape=[jax.ShapeDtypeStruct((count, width_q), BF), jax.ShapeDtypeStruct(kv.shape, BF)],
        compiler_params=MEMORY,
        cost_estimate=FREE,
    )(size, q, kv, do, lse, positions, key_positions, cosine, sine)


def leave_kernel(x_ref, o_ref, weight_ref, gain_ref, h_ref, n_ref):
    mixed = x_ref[...].astype(F32) + matmul(o_ref[...], weight_ref[...])
    h_ref[...] = mixed
    n_ref[...] = (mixed * mean_scale(mixed) * gain_ref[...]).astype(BF)


def leave_pass(x, o, weight, gain):
    count, width = x.shape
    tile = count // 2
    return pl.pallas_call(
        leave_kernel,
        grid=(count // tile,),
        in_specs=[strip(tile, width), strip(tile, o.shape[1]), held(weight), held(gain)],
        out_specs=[strip(tile, width)] * 2,
        out_shape=[jax.ShapeDtypeStruct((count, width), d) for d in (F32, BF)],
        compiler_params=MEMORY,
        cost_estimate=FREE,
    )(x, o, weight, gain)


def norm_grad(grad, values, gain):
    scaling = mean_scale(values)
    unit = values * scaling
    lifted = grad * gain
    back = scaling * (lifted - unit * jnp.mean(lifted * unit, axis=-1, keepdims=True))
    return back, jnp.sum(grad * unit, axis=0, keepdims=True)


def add_step(ref, value):
    @pl.when(pl.program_id(0) == 0)
    def _():
        ref[...] = value

    @pl.when(pl.program_id(0) > 0)
    def _():
        ref[...] += value


def leave_back_kernel(
    one_ref, two_ref, h_ref, gain_ref, dy_ref, weight_ref, dh_ref, dz_ref, do_ref, dgain_ref
):
    grad = one_ref[...].astype(F32) + two_ref[...].astype(F32)
    back, gain_sum = norm_grad(grad, h_ref[...], gain_ref[...])
    total = dy_ref[...].astype(F32) + back
    dh_ref[...] = total
    low = total.astype(BF)
    dz_ref[...] = low
    do_ref[...] = through(low, weight_ref[...]).astype(BF)
    add_step(dgain_ref, gain_sum)


def leave_back_pass(one, two, h, gain, dy, weight):
    count, width = h.shape
    tile = count // 2
    width_q = weight.shape[0]
    return pl.pallas_call(
        leave_back_kernel,
        grid=(count // tile,),
        in_specs=[strip(tile, width)] * 3 + [held(gain), strip(tile, width), held(weight)],
        out_specs=[strip(tile, width)] * 2
        + [strip(tile, width_q), pl.BlockSpec((1, width), lambda i: (0, 0))],
        out_shape=[
            jax.ShapeDtypeStruct((count, width), F32),
            jax.ShapeDtypeStruct((count, width), BF),
            jax.ShapeDtypeStruct((count, width_q), BF),
            jax.ShapeDtypeStruct((1, width), F32),
        ],
        compiler_params=MEMORY,
        cost_estimate=FREE,
    )(one, two, h, gain, dy, weight)


def enter_back_kernel(dq_ref, *refs):
    parts = refs[:-9]
    cos_ref, sin_ref, weight_ref, x_ref, gain_ref, dh_ref, joined_ref, dx_ref, dgain_ref = refs[-9:]
    head = parts[0].shape[1] // 2
    width_q = dq_ref.shape[1]
    pair = parts[0][...].astype(F32)
    for part in parts[1:]:
        pair = pair + part[...].astype(F32)
    joined_ref[:, :width_q] = dq_ref[...]
    spun = turned(pair[:, :head], cos_ref[...], -sin_ref[...])
    joined_ref[:, width_q : width_q + head] = spun.astype(BF)
    joined_ref[:, width_q + head :] = pair[:, head:].astype(BF)
    grad = through(joined_ref[...], weight_ref[...])
    back, gain_sum = norm_grad(grad, x_ref[...].astype(F32), gain_ref[...])
    dx_ref[...] = (dh_ref[...] + back).astype(BF)
    add_step(dgain_ref, gain_sum)


def enter_back_pass(dq, parts, cosine, sine, weight, x, gain, dh):
    count, width = x.shape
    tile = count // 2
    width_q = dq.shape[1]
    return pl.pallas_call(
        enter_back_kernel,
        grid=(count // tile,),
        in_specs=[strip(tile, width_q)]
        + [strip(tile, part.shape[1]) for part in parts]
        + [strip(tile, cosine.shape[1])] * 2
        + [held(weight), strip(tile, width), held(gain), strip(tile, width)],
        out_specs=[
            strip(tile, weight.shape[1]),
            strip(tile, width),
            pl.BlockSpec((1, width), lambda i: (0, 0)),
        ],
        out_shape=[
            jax.ShapeDtypeStruct((count, weight.shape[1]), BF),
            jax.ShapeDtypeStruct((count, width), BF),
            jax.ShapeDtypeStruct((1, width), F32),
        ],
        compiler_params=MEMORY,
        cost_estimate=FREE,
    )(dq, *parts, cosine, sine, weight, x, gain, dh)


def halving_order(bits):
    order = [0]
    for bit in reversed(bits):
        order = order + [flip | bit for flip in order]
    return order


def ff_kernel(n2_ref, df_ref, wg_ref, wd_ref, a_ref, dg_ref, dn_ref):
    hidden = wd_ref.shape[0]
    n2 = n2_ref[...]
    gate = matmul(n2, wg_ref[:, :hidden])
    upper = matmul(n2, wg_ref[:, hidden:])
    grad = through(df_ref[...], wd_ref[...])
    square = gate * gate
    bent = jnp.tanh(gate * (ROOT + ROOT * CUBE * square))
    half = 0.5 + 0.5 * bent
    act = gate * half
    a_ref[...] = (act * upper).astype(BF)
    slope = half + 0.5 * gate * (1.0 - bent * bent) * (ROOT + 3.0 * ROOT * CUBE * square)
    dg_ref[:, :hidden] = (grad * upper * slope).astype(BF)
    dg_ref[:, hidden:] = (grad * act).astype(BF)
    dn_ref[...] = through(dg_ref[...], wg_ref[...]).astype(BF)


def ff_pass(n2, df, wg, wd, tile):
    count, width = n2.shape
    hidden = wd.shape[0]

    return pl.pallas_call(
        ff_kernel,
        grid=(count // tile,),
        in_specs=[strip(tile, width), strip(tile, width), held(wg), held(wd)],
        out_specs=[strip(tile, hidden), strip(tile, 2 * hidden), strip(tile, width)],
        out_shape=[
            jax.ShapeDtypeStruct((count, hidden), BF),
            jax.ShapeDtypeStruct((count, 2 * hidden), BF),
            jax.ShapeDtypeStruct((count, width), BF),
        ],
        compiler_params=MEMORY,
        cost_estimate=FREE,
    )(n2, df, wg, wd)


def blocks_of(padded, width, columns):
    across = columns // 128
    wide = width // 128
    out = []
    for r in range(padded // 16):
        for c in range(wide):
            out.append((16 * r, 128 * c, 16 * ((r * wide + c) // across), 128 * ((r * wide + c) % across)))
    return out, 16 * (-(-len(out) // across))


def tall(value, height):
    short = height - value.shape[0]
    if not short:
        return value
    return jnp.concatenate([value, jnp.zeros((short, value.shape[1]), value.dtype)], axis=0)


def deal_kernel(piece, padded, *refs):
    gateup_ref, leave_ref, out_ref = refs[0], refs[1], refs[-1]
    team, total, columns = out_ref.shape
    units, shard = gateup_ref.shape[1] // 2, columns // 2
    lines = leave_ref.shape[0]
    for in_ref, row in ((leave_ref, 0), (gateup_ref, total - gateup_ref.shape[0])):
        height = in_ref.shape[0]
        gap = jnp.zeros((height, padded - piece), in_ref.dtype)
        for half in range(2):
            for seat in range(team):
                parts = []
                for block in range(shard // padded):
                    start = half * units + (block * team + seat) * piece
                    parts += [in_ref[:, start : start + piece], gap]
                joined = jnp.concatenate(parts, axis=1)
                out_ref[seat, row : row + height, half * shard : (half + 1) * shard] = joined
    if len(refs) == 4:
        rank = refs[2].shape[1]
        for seat in range(team):
            for row in range(0, padded, 16):
                first = seat * piece + row
                value = tall(refs[2][first : first + min(16, piece - row), :], 16)
                start = row // 16 * rank
                out_ref[seat, lines : lines + 16, start : start + rank] = value


def deal_pass(arrays, team, piece, padded):
    lines = sum(array.shape[0] for array in arrays[:2]) + 16 * (len(arrays) == 3)
    columns = arrays[0].shape[1] // (team * piece) * padded
    return pl.pallas_call(
        lambda *refs: deal_kernel(piece, padded, *refs),
        out_shape=jax.ShapeDtypeStruct((team, lines, columns), BF),
        compiler_params=MEMORY,
        cost_estimate=FREE,
    )(*arrays)


def slab_kernel(padded, dealt_ref, down_ref, slab_ref, rest_ref):
    team, total, columns = dealt_ref.shape
    lines = rest_ref.shape[1]
    height = total - lines
    piece, width = down_ref.shape
    base = team * height
    for seat in range(team):
        slab_ref[seat * height : (seat + 1) * height, :] = dealt_ref[seat, lines:total, :]
        rest_ref[seat] = dealt_ref[seat, :lines, :]
    where, extra = blocks_of(padded, width, columns)
    slab_ref[base + extra - 16 : base + extra, :] = jnp.zeros((16, columns), BF)
    for r, c, row, lane in where:
        value = tall(down_ref[r : r + min(16, piece - r), c : c + 128], 16)
        slab_ref[base + row : base + row + 16, lane : lane + 128] = value


def slab_pass(dealt, down, lines, padded):
    team, total, columns = dealt.shape
    extra = blocks_of(padded, down.shape[1], columns)[1]
    return pl.pallas_call(
        lambda *refs: slab_kernel(padded, *refs),
        out_shape=[
            jax.ShapeDtypeStruct((team * (total - lines) + extra, columns), BF),
            jax.ShapeDtypeStruct((team, lines, columns), BF),
        ],
        compiler_params=MEMORY,
        cost_estimate=FREE,
    )(dealt, down)


def assemble_kernel(lines, side_ref, near_ref, far_ref, *outs):
    team = near_ref.shape[0]

    def fill(half, ref):
        for seat in range(team):
            first = (half * team + seat) * lines
            outs[0][first : first + lines, :] = ref[seat, :lines, :]
            if len(outs) == 2:
                rank = outs[1].shape[1]
                padded = outs[1].shape[0] // (2 * team)
                for row in range(0, padded, 16):
                    start = row // 16 * rank
                    first = (half * team + seat) * padded + row
                    outs[1][first : first + 16, :] = ref[
                        seat, lines : lines + 16, start : start + rank
                    ]

    for half in range(2):

        @pl.when(side_ref[0] == half)
        def _(half=half):
            fill(half, near_ref)
            fill(1 - half, far_ref)


def assemble_pass(side, near, far, lines, shard, rank):
    team, height, columns = near.shape
    shapes = [jax.ShapeDtypeStruct((2 * team * lines, columns), BF)]
    if height > lines:
        shapes.append(jax.ShapeDtypeStruct((shard, rank), BF))
    vmem = pl.BlockSpec(memory_space=pltpu.VMEM)
    return pl.pallas_call(
        lambda *refs: assemble_kernel(lines, *refs),
        in_specs=[pl.BlockSpec(memory_space=pltpu.SMEM), vmem, vmem],
        out_specs=[vmem] * len(shapes),
        out_shape=shapes,
        compiler_params=MEMORY,
        cost_estimate=FREE,
    )(side, near, far)


def fold_ff_kernel(order_ref, *refs):
    slabs = refs[:-7]
    enter_ref, leave_ref, down_enter_ref, down_leave_ref, gateup_out, down_out, blocks = refs[-7:]
    rank = leave_ref.shape[0]
    height, columns = gateup_out.shape
    shard = columns // 2
    step = pl.program_id(0)
    for index in range(2):
        start = index * shard
        lift = matmul(
            enter_ref[:, index * rank : (index + 1) * rank], leave_ref[:, start : start + shard]
        )
        for which, slab_ref in enumerate(slabs):

            @pl.when(step == which)
            def _(slab_ref=slab_ref, lift=lift, start=start):
                part = slab_ref[:height, start : start + shard].astype(F32)
                gateup_out[:, start : start + shard] = (part + lift).astype(BF)

    for which, slab_ref in enumerate(slabs):

        @pl.when(step == which)
        def _(slab_ref=slab_ref):
            blocks[...] = slab_ref[height:, :]

    lift = matmul(down_enter_ref[...], down_leave_ref[...])
    padded, width = down_out.shape
    wide = width // 128
    where, _ = blocks_of(padded, width, columns)
    for first in range(0, len(where), wide):
        r = where[first][0]
        parts = [
            blocks[row : row + 16, lane : lane + 128]
            for _, _, row, lane in where[first : first + wide]
        ]
        part = jnp.concatenate(parts, axis=1).astype(F32)
        down_out[r : r + 16, :] = (part + lift[r : r + 16]).astype(BF)


def fold_ff_pass(order, slabs, enter, leave, down_enter, down_leave, padded):
    count = len(slabs)
    columns, width = leave.shape[1], down_leave.shape[1]
    height = enter.shape[0] // count

    def own(rows, wide):
        return pl.BlockSpec((rows, wide), lambda i, o: (o[i], 0))

    return pl.pallas_call(
        fold_ff_kernel,
        grid_spec=pltpu.PrefetchScalarGridSpec(
            num_scalar_prefetch=1,
            grid=(count,),
            in_specs=[held(slab) for slab in slabs]
            + [
                own(height, enter.shape[1]),
                held(leave),
                own(padded, down_enter.shape[1]),
                held(down_leave),
            ],
            out_specs=[own(height, columns), own(padded, width)],
            scratch_shapes=[pltpu.VMEM((slabs[0].shape[0] - height, columns), BF)],
        ),
        out_shape=[
            jax.ShapeDtypeStruct((count * height, columns), BF),
            jax.ShapeDtypeStruct((count * padded, width), BF),
        ],
        compiler_params=MEMORY,
        cost_estimate=FREE,
    )(order, *slabs, enter, leave, down_enter, down_leave)


def fold_attn_kernel(bands, order_ref, *refs):
    slabs = refs[:-6]
    enter_ref, leave_ref, out_enter_ref, out_leave_ref, in_out, out_out = refs[-6:]
    rank = leave_ref.shape[0]
    height, width = in_out.shape[0], out_out.shape[1]
    step = pl.program_id(0)
    lifts = [
        matmul(enter_ref[:, i * rank : (i + 1) * rank], leave_ref[:, start : start + size])
        for i, (start, size) in enumerate(bands)
    ]
    out_lift = matmul(out_enter_ref[...], out_leave_ref[...])
    for which, slab_ref in enumerate(slabs):

        @pl.when(step == which)
        def _(slab_ref=slab_ref):
            for (start, size), lift in zip(bands, lifts):
                part = slab_ref[:height, start : start + size].astype(F32)
                in_out[:, start : start + size] = (part + lift).astype(BF)
            part = slab_ref[height:, :width].astype(F32)
            out_out[...] = (part + out_lift).astype(BF)


def fold_attn_pass(order, slabs, enter, leave, out_enter, out_leave, bands):
    count = len(slabs)
    height, short = enter.shape[0] // count, out_enter.shape[0] // count

    def own(rows, wide):
        return pl.BlockSpec((rows, wide), lambda i, o: (o[i], 0))

    return pl.pallas_call(
        lambda *refs: fold_attn_kernel(bands, *refs),
        grid_spec=pltpu.PrefetchScalarGridSpec(
            num_scalar_prefetch=1,
            grid=(count,),
            in_specs=[held(slab) for slab in slabs]
            + [
                own(height, enter.shape[1]),
                held(leave),
                own(short, out_enter.shape[1]),
                held(out_leave),
            ],
            out_specs=[own(height, leave.shape[1]), own(short, out_leave.shape[1])],
        ),
        out_shape=[
            jax.ShapeDtypeStruct((enter.shape[0], leave.shape[1]), BF),
            jax.ShapeDtypeStruct((out_enter.shape[0], out_leave.shape[1]), BF),
        ],
        compiler_params=MEMORY,
        cost_estimate=FREE,
    )(order, *slabs, enter, leave, out_enter, out_leave)


def slabs_out_kernel(order_ref, gateup_ref, down_ref, out_ref):
    height, columns = gateup_ref.shape
    padded, width = down_ref.shape
    out_ref[0, :height, :] = gateup_ref[...]
    where, extra = blocks_of(padded, width, columns)
    out_ref[0, height + extra - 16 :, :] = jnp.zeros((16, columns), BF)
    for r, c, row, lane in where:
        value = down_ref[r : r + 16, c : c + 128]
        out_ref[0, height + row : height + row + 16, lane : lane + 128] = value


def slabs_out_pass(order, gateup, down, parts):
    columns, width = gateup.shape[1], down.shape[1]
    height, padded = gateup.shape[0] // parts, down.shape[0] // parts
    rows = height + blocks_of(padded, width, columns)[1]
    count = order.shape[0]
    return pl.pallas_call(
        slabs_out_kernel,
        grid_spec=pltpu.PrefetchScalarGridSpec(
            num_scalar_prefetch=1,
            grid=(count,),
            in_specs=[
                pl.BlockSpec((height, columns), lambda i, o: (o[i], 0)),
                pl.BlockSpec((padded, width), lambda i, o: (o[i], 0)),
            ],
            out_specs=pl.BlockSpec((1, rows, columns), lambda i, o: (i, 0, 0)),
        ),
        out_shape=jax.ShapeDtypeStruct((count, rows, columns), BF),
        compiler_params=MEMORY,
        cost_estimate=FREE,
    )(order, gateup, down)


def sides_kernel(order_ref, *refs):
    enters, grad_ref = refs[:4], refs[4]
    downs = refs[5:-2]
    lines = 2 * enters[0].shape[1]
    shard = grad_ref.shape[1] // 2
    for side, out_ref in enumerate(refs[-2:]):
        team = out_ref.shape[0]
        lines = enters[0].shape[1] // team
        for half in range(2):
            value = outer_sum(
                enters[2 * half + side][...], grad_ref[:, half * shard : (half + 1) * shard]
            ).astype(BF)
            for seat in range(team):
                out_ref[seat, :lines, half * shard : (half + 1) * shard] = value[
                    seat * lines : (seat + 1) * lines
                ]
        if downs:
            value = through(downs[side][...], downs[2][...]).astype(BF)
            rank = value.shape[1]
            padded = value.shape[0] // team
            for seat in range(team):
                for row in range(0, padded, 16):
                    start = row // 16 * rank
                    first = seat * padded + row
                    out_ref[seat, lines : lines + 16, start : start + rank] = value[
                        first : first + 16
                    ]


def sides_pass(order, enter, grad, down, down_leave, team, together):
    width, columns = grad.shape
    half = enter.shape[1] // 4

    def near_or_far(rows, wide, at):
        return pl.BlockSpec((rows, wide), at)

    specs = [
        pl.BlockSpec((width, half), lambda i, o: (0, o[0])),
        pl.BlockSpec((width, half), lambda i, o: (0, o[1])),
        pl.BlockSpec((width, half), lambda i, o: (0, 2 + o[0])),
        pl.BlockSpec((width, half), lambda i, o: (0, 2 + o[1])),
        held(grad),
    ]
    arrays = [enter] * 4 + [grad]
    lines = half // team
    if together:
        lines += 16
        rows = down.shape[0] // 2
        specs += [
            pl.BlockSpec((rows, down.shape[1]), lambda i, o: (o[0], 0)),
            pl.BlockSpec((rows, down.shape[1]), lambda i, o: (o[1], 0)),
            held(down_leave),
        ]
        arrays += [down, down, down_leave]
    shape = (team, lines, columns)
    return pl.pallas_call(
        sides_kernel,
        grid_spec=pltpu.PrefetchScalarGridSpec(
            num_scalar_prefetch=1,
            grid=(1,),
            in_specs=specs,
            out_specs=[pl.BlockSpec(shape, lambda i, o: (0, 0, 0))] * 2,
        ),
        out_shape=[jax.ShapeDtypeStruct(shape, BF)] * 2,
        compiler_params=MEMORY,
        cost_estimate=FREE,
    )(order, *arrays)


def home_kernel(piece, near_ref, far_ref, mine_ref, other_ref, dealt_ref, down_ref):
    team, total, columns = dealt_ref.shape
    lines = mine_ref.shape[1]
    height = total - lines
    base = team * height
    for seat in range(team):
        rest = mine_ref[seat].astype(F32) + other_ref[seat].astype(F32)
        dealt_ref[seat, :lines, :] = rest.astype(BF)
        rows = slice(seat * height, (seat + 1) * height)
        value = near_ref[rows, :].astype(F32) + far_ref[rows, :].astype(F32)
        dealt_ref[seat, lines:total, :] = value.astype(BF)
    width = down_ref.shape[1]
    for r, c, row, lane in blocks_of(even(piece), width, columns)[0]:
        rows, lanes = slice(base + row, base + row + 16), slice(lane, lane + 128)
        value = near_ref[rows, lanes].astype(F32) + far_ref[rows, lanes].astype(F32)
        size = min(16, piece - r)
        down_ref[r : r + size, c : c + 128] = value[:size]


def home_pass(near, far, mine, other, piece, width, height):
    team, lines, columns = mine.shape
    return pl.pallas_call(
        lambda *refs: home_kernel(piece, *refs),
        out_shape=[
            jax.ShapeDtypeStruct((team, lines + height, columns), BF),
            jax.ShapeDtypeStruct((piece, width), F32),
        ],
        compiler_params=MEMORY,
        cost_estimate=FREE,
    )(near, far, mine, other)


def join_kernel(piece, padded, in_ref, *outs):
    team, total, columns = in_ref.shape
    units, shard = outs[0].shape[1] // 2, columns // 2
    lines = outs[0].shape[0]
    for out_ref, row in ((outs[0], 0), (outs[1], total - outs[1].shape[0])):
        height = out_ref.shape[0]
        for half in range(2):
            for block in range(shard // padded):
                first = half * shard + block * padded
                parts = [
                    in_ref[seat, row : row + height, first : first + piece] for seat in range(team)
                ]
                start = half * units + block * team * piece
                joined = jnp.concatenate(parts, axis=1).astype(F32)
                out_ref[:, start : start + team * piece] = joined
    if len(outs) == 3:
        rank = outs[2].shape[1]
        for seat in range(team):
            for row in range(0, padded, 16):
                size = min(16, piece - row)
                start = row // 16 * rank
                value = in_ref[seat, lines : lines + size, start : start + rank]
                first = seat * piece + row
                outs[2][first : first + size, :] = value.astype(F32)


def join_pass(parts, lines, height, piece, padded, rank):
    team, total, columns = parts.shape
    wide = columns // padded * piece * team
    shapes = [(lines, wide), (height, wide)]
    if total > lines + height:
        shapes.append((team * piece, rank))
    return pl.pallas_call(
        lambda *refs: join_kernel(piece, padded, *refs),
        out_shape=[jax.ShapeDtypeStruct(shape, F32) for shape in shapes],
        compiler_params=MEMORY,
        cost_estimate=FREE,
    )(parts)


def per_device(
    tokens,
    cotangent,
    exit_depth,
    lengths,
    loop_index,
    attn_gain,
    mlp_gain,
    qkv_weight,
    out_weight,
    gateup_weight,
    down_weight,
    qkv_enter,
    query_leave,
    kv_leave,
    out_enter,
    out_leave,
    gateup_enter,
    gateup_leave,
    down_enter,
    down_leave,
):
    loops = lax.axis_size("depth")
    rows = lax.axis_size("rows")
    group = lax.axis_index("depth")
    place = lax.axis_index("rows")
    slots, seq_dev, width = tokens.shape
    sub = rows // slots
    team = rows // 2
    count = slots * seq_dev
    teams = [[h * team + k for k in range(team)] for h in range(2)]
    seq_here, mate, core = place // sub, place % sub, place % 2
    side, seat = place // team, place % team
    levels = jnp.arange(loops, dtype=jnp.int32)

    head = kv_leave.shape[2] // 2
    width_q = query_leave.shape[2]
    rank = qkv_enter.shape[2] // 3
    hidden_units = gateup_weight.shape[1] // 2
    piece = down_weight.shape[0]
    padded = -(-piece // 16) * 16
    shard = 2 * loops * padded
    slab = width // (2 * loops)
    gain_size = attn_gain.shape[0]

    def turn(values):
        return jnp.stack(
            [values[0]] + [swap(values[f], "rows", f * sub) for f in range(1, slots)]
        )

    def deal(values):
        return lax.all_to_all(
            values, "rows", split_axis=0, concat_axis=0, axis_index_groups=teams, tiled=True
        )

    def pick(array, index):
        return array.at[index].get(mode="promise_in_bounds")

    def halve(array, bit):
        half = array.shape[0] // 2
        return array[:half], swap(array[half:], "rows", bit)

    def halve_but_last(array, bits):
        for bit in bits[:-1]:
            array = add_low(*halve(array, bit))
        return array

    def own_half(array, which):
        height = array.shape[0] // 2
        return lax.dynamic_slice(array, (which * height, 0), (height, array.shape[1]))

    def positions_of(who):
        blocks = (seq_here ^ levels) * sub + who
        return (blocks[:, None] * seq_dev + jnp.arange(seq_dev, dtype=jnp.int32)[None, :]).reshape(
            count
        )

    depth_flips = [0, 1, 2, 3]
    halves_order = jnp.stack([(group ^ f) * 2 + (core ^ e) for f in depth_flips for e in (0, 1)])
    flips = [(d, f) for d in range(4) for f in range(2)]
    slab_at = {(d, f): (group ^ d) * 2 + (side ^ f) for d, f in flips}
    team_bits, sub_bits, row_bits = bits_of(team), bits_of(sub), bits_of(rows)
    bands = [(0, width_q), (width_q, head), (width_q + head, head)]
    together = team == loops
    lines = gateup_leave.shape[1]
    with_enter = lines + 16 if together else lines

    table = loop_index.reshape(loops, loops)
    mine = lax.dynamic_index_in_dim(table, group, 0, keepdims=False)
    order = jnp.sum((mine[None, :] == levels[:, None]).astype(jnp.int32) * levels[None, :], axis=1)
    sizes_here = jnp.sum(jnp.where(table == group, lengths.reshape(loops, loops), 0), axis=1)
    size_here = lax.dynamic_slice(sizes_here, (seq_here,), (1,))
    positions = positions_of(mate)
    cosine, sine = angles(positions.astype(F32), head)
    gains = jnp.concatenate([attn_gain, mlp_gain])[None]
    gains = jnp.concatenate([gains] + [swap(gains, "depth", f) for f in depth_flips[1:]])
    gains = pick(gains, group ^ levels)
    small = [
        qkv_weight,
        qkv_enter[0],
        jnp.concatenate([query_leave[0], kv_leave[0]], axis=1),
        out_weight,
        out_enter[0],
        out_leave[0],
        gains,
    ]
    small_shapes = [array.shape for array in small]
    late = [gateup_enter[0], down_leave[0]]
    late_shapes = [array.shape for array in late]
    late_packed = pack_pass(late)
    packed = lax.all_gather(pack_pass(small), "rows", axis=0, tiled=True)
    arrived = lax.all_to_all(
        pick(tokens, order), "depth", split_axis=0, concat_axis=0, tiled=True
    )
    dealt = deal_pass(
        [gateup_weight, gateup_leave[0]] + [down_enter[0]] * together, team, piece, padded
    )
    upstream_low = turn(pick(cotangent, seq_here ^ levels)).reshape(count, width)
    arrived, dealt, upstream_low = tie(arrived, dealt, upstream_low)
    inputs = turn(pick(arrived, seq_here ^ levels)).reshape(count, width)
    dealt = deal(dealt)
    inputs, dealt, packed, upstream_low = tie(inputs, dealt, packed, upstream_low)

    slab_near, rest_near = slab_pass(dealt, down_weight, with_enter, padded)
    slab_far = swap(slab_near, "rows", team)
    (
        qkv_slab,
        full_qkv_enter,
        full_leave,
        out_slab,
        full_out_enter,
        full_out_leave,
        gain_slab,
    ) = unpack_pass(packed, small_shapes, BF)
    gain_slab = gain_slab.reshape(rows, loops, 2, -1)
    both_gains = gain_slab.transpose(2, 1, 0, 3).reshape(2, 1, width).astype(F32)
    gain_one, gain_two = both_gains[0], both_gains[1]
    spare = qkv_slab.shape[1] - width

    def both_halves(which):
        return jnp.concatenate(
            [own_half(qkv_slab, which), jnp.pad(own_half(out_slab, which), ((0, 0), (0, spare)))]
        )

    half_here = both_halves(core)
    fetched = [swap(half_here, "depth", f) for f in depth_flips[1:]]
    fetched, slab_near, slab_far, upstream_low, rest_near = tie(
        fetched, slab_near, slab_far, upstream_low, rest_near
    )
    others = swap(jnp.stack(fetched), "rows", 1)
    others, slab_near, rest_near, late_packed = tie(others, slab_near, rest_near, late_packed)
    late_packed = lax.all_gather(late_packed, "rows", axis=0, tiled=True)
    rest_far = swap(rest_near, "rows", team)
    slabs = {(0, 0): slab_near, (0, 1): slab_far}
    slabs[(1, 0)] = swap(slab_near, "depth", 1)
    slabs[(2, 0)] = swap(slab_near, "depth", 2)
    slabs[(1, 1)] = swap(slab_far, "depth", 1)
    slabs[(2, 1)] = swap(slab_far, "depth", 2)
    halves = [half_here, both_halves(core ^ 1)]
    for f in range(3):
        halves += [fetched[f], others[f]]
    qkv_eff, out_eff = fold_attn_pass(
        halves_order, halves, full_qkv_enter, full_leave, full_out_enter, full_out_leave, bands
    )
    normed_one, queries, pairs_all = enter_pass(
        inputs, gain_one, qkv_eff, cosine, sine, width_q
    )
    pairs_all, rest_far, slabs, upstream_low = tie(pairs_all, rest_far, slabs, upstream_low)
    cotan_far = swap(upstream_low, "rows", team_bits[-1])
    slabs[(3, 0)] = swap(slabs[(1, 0)], "depth", 2)
    slabs[(3, 1)] = swap(slabs[(2, 1)], "depth", 1)
    mates = [0]
    for bit in sub_bits:
        pairs_all = jnp.concatenate([pairs_all, swap(pairs_all, "rows", bit)])
        mates = mates + [f | bit for f in mates]
    key_pos = jnp.concatenate([positions_of(mate ^ f) for f in mates])[None]
    attended, log_total = attend_pass(
        size_here, queries, pairs_all, positions[:, None], key_pos, seq_dev
    )
    mixed, normed_two = leave_pass(inputs, attended, out_eff, gain_two)
    normed_two, slabs, cotan_far = tie(normed_two, slabs, cotan_far)

    def gather_team(value, far):
        value = jnp.concatenate([value, far])
        for bit in team_bits[-2::-1]:
            value = jnp.concatenate([value, swap(value, "rows", bit)])
        return value

    normed_far = swap(normed_two, "rows", team_bits[-1])
    full_gateup_enter, full_down_leave = unpack_pass(late_packed, late_shapes, BF)
    leave_full, *enter_full = assemble_pass(
        side[None], rest_near, rest_far, lines, shard, rank
    )
    if together:
        enter_full = enter_full[0]
    else:
        enter_every = lax.all_gather(down_enter[0], "rows", axis=0, tiled=True)
        enter_every = enter_every.reshape(loops, 2, team, piece, rank)
        enter_full = lax.dynamic_index_in_dim(enter_every, seat, 2, keepdims=False)
        enter_full = jnp.pad(enter_full, ((0, 0), (0, 0), (0, padded - piece), (0, 0)))
        enter_full = enter_full.reshape(shard, rank)
    gateup_eff, down_eff = fold_ff_pass(
        jnp.stack([slab_at[f] for f in flips]),
        [slabs[f] for f in flips],
        full_gateup_enter,
        leave_full,
        enter_full,
        full_down_leave,
        padded,
    )
    normed_far, gateup_eff, down_eff = tie(normed_far, gateup_eff, down_eff)
    cotan_team = gather_team(upstream_low, cotan_far)
    normed_team = gather_team(normed_two, normed_far)

    hidden, grad_expanded, grad_normed = ff_pass(
        normed_team, cotan_team, gateup_eff, down_eff, 256
    )

    grad_normed = halve_but_last(grad_normed, team_bits)
    grad_normed, hidden, grad_expanded = tie(grad_normed, hidden, grad_expanded)
    grad_terms = halve(grad_normed, team_bits[-1])
    grad_gateup = outer_sum(normed_team, grad_expanded).astype(BF)
    grad_down = outer_sum(hidden, cotan_team).astype(BF)
    grad_terms, grad_gateup, grad_down, hidden = tie(grad_terms, grad_gateup, grad_down, hidden)

    def slabs_out(*which):
        index = jnp.stack([slab_at[f] for f in which])
        return slabs_out_pass(index, grad_gateup, grad_down, 2 * loops)

    near_sent, far_sent = slabs_out((2, 0), (3, 0)), slabs_out((1, 1), (3, 1))
    near_sent, far_sent, grad_gateup, grad_down = tie(
        near_sent, far_sent, grad_gateup, grad_down
    )
    near_got = swap(near_sent, "depth", 2)
    far_got = swap(far_sent, "depth", 1)
    sides = jnp.stack([side, side ^ 1])
    side_near, side_far = sides_pass(
        sides, full_gateup_enter, grad_gateup, grad_down, full_down_leave, team, together
    )
    side_near, side_far, grad_terms, hidden = tie(side_near, side_far, grad_terms, hidden)
    side_got = swap(side_far, "rows", team)
    grad_mixed, grad_branch, grad_attended, grad_gain_second = leave_back_pass(
        *grad_terms, mixed, gain_two, upstream_low, out_eff
    )
    grad_queries, key_terms = attend_back_pass(
        size_here,
        queries,
        pairs_all,
        grad_attended,
        log_total,
        positions[:, None],
        key_pos,
        cosine,
        sine,
        seq_dev,
    )
    mate_order = halving_order(sub_bits)
    if mate_order != mates:
        key_terms = jnp.concatenate(
            [key_terms[i * count : (i + 1) * count] for i in map(mates.index, mate_order)]
        )
    outcome = matmul(hidden, down_eff).astype(BF)
    near_kept, far_kept = slabs_out((0, 0), (1, 0)), slabs_out((0, 1), (2, 1))
    key_terms, grad_queries, near_got, far_got, outcome, near_kept, far_kept, side_got = tie(
        key_terms, grad_queries, near_got, far_got, outcome, near_kept, far_kept, side_got
    )
    pair_terms = halve(halve_but_last(key_terms, sub_bits), sub_bits[-1])
    outcome = halve_but_last(outcome, team_bits)
    pair_terms, outcome = tie(pair_terms, outcome)

    grad_joined, grad_inputs, grad_gain_first = enter_back_pass(
        grad_queries, pair_terms, cosine, sine, qkv_eff, inputs, gain_one, grad_mixed
    )
    near_one, far_one = add_low(near_kept[1], near_got[1]), add_low(far_kept[1], far_got[1])
    near_one, far_one = swap(near_one, "depth", 1), swap(far_one, "depth", 2)
    outcome = halve(outcome, team_bits[-1])
    grad_qkv = outer_sum(normed_one, grad_joined).astype(BF)
    grad_out = outer_sum(attended, grad_branch).astype(BF)

    near_one, far_one, outcome, grad_inputs, grad_qkv, grad_out = tie(
        near_one, far_one, outcome, grad_inputs, grad_qkv, grad_out
    )

    def loop_part(flip):
        parts = []
        for array in (grad_qkv, grad_out):
            height = array.shape[0] // loops
            part = lax.dynamic_slice(array, ((group ^ flip) * height, 0), (height, array.shape[1]))
            parts.append(jnp.pad(part, ((0, 0), (0, grad_qkv.shape[1] - array.shape[1]))))
        return jnp.concatenate(parts)

    terms = [loop_part(0)] + [swap(loop_part(f), "depth", f) for f in depth_flips[1:]]
    near_sum = add_low(near_kept[0], near_got[0])
    far_sum = add_low(far_kept[0], far_got[0])
    result = mixed + (outcome[0].astype(F32) + outcome[1].astype(F32))
    result_low = result.astype(BF)
    near_sum, far_sum = add_low(near_sum, near_one), add_low(far_sum, far_one)
    far_sum = swap(far_sum, "rows", team)
    result_low, grad_qkv, grad_out, near_sum, far_sum, terms = tie(
        result_low, grad_qkv, grad_out, near_sum, far_sum, terms
    )

    dealt, grad_down_weight = home_pass(
        near_sum, far_sum, side_near, side_got, piece, width, slab // team
    )
    homeward = jnp.concatenate(
        [result_low.reshape(slots, seq_dev, width), grad_inputs.reshape(slots, seq_dev, width)],
        axis=1,
    )

    homeward, dealt = tie(homeward, dealt)
    homeward = turn(homeward)
    dealt = deal(dealt)
    row_place = jnp.arange(rows, dtype=jnp.int32)

    def to_owner(packed):
        return lax.psum_scatter(packed, "rows", scatter_dimension=0, tiled=True)

    qkv_rows = grad_qkv.shape[0] // loops
    rest_grads_of = [
        ((terms[0].shape[0] - qkv_rows) // rows, width),
        (grad_out.shape[0] // rows, rank),
        (rank // rows, width),
        (width // rows, rank),
        (width // rows, rank),
        (rank // rows, width),
    ]
    rest_sum = grads_pass(
        lambda *refs: rest_grads_kernel(qkv_rows, *refs),
        row_place,
        rows,
        rest_grads_of,
        [
            *terms,
            grad_out,
            full_out_enter,
            full_out_leave,
            grad_gateup,
            leave_full,
            grad_down,
            enter_full,
        ],
    )
    rest_sum = to_owner(rest_sum)
    attn_grads_of = attn_grads_shapes(rows, qkv_rows, grad_qkv, full_qkv_enter, full_leave, bands)
    attn_sum = grads_pass(
        lambda *refs: attn_grads_kernel(qkv_rows, bands, *refs),
        row_place,
        rows,
        attn_grads_of,
        [*terms, grad_qkv, full_qkv_enter, full_leave],
    )
    attn_sum = to_owner(attn_sum)
    homeward, dealt = tie(homeward, dealt)
    returned = lax.all_to_all(
        pick(homeward[:, seq_dev:], seq_here ^ levels),
        "depth",
        split_axis=0,
        concat_axis=0,
        tiled=True,
    )

    grad_tokens = pick(returned, mine)
    activations = pick(homeward[:, :seq_dev], seq_here ^ levels)
    own_out, *rest_grads = unpack_pass(
        rest_sum, rest_grads_of, F32, [[0], [1], [2], [3, 4], [5]]
    )
    own_qkv, *attn_grads = unpack_pass(
        attn_sum, attn_grads_of, F32, [[0], [1, 2, 3], [4], [5, 6]]
    )
    grad_gateup_leave, grad_gateup_weight, *grad_down_enter = join_pass(
        dealt, lines, slab // team, piece, padded, rank
    )
    if together:
        grad_down_enter = grad_down_enter[0]
    else:
        grad_down_in = through(grad_down, full_down_leave).astype(BF)
        grad_down_in = grad_down_in.reshape(loops, 2, 1, padded, rank)[:, :, :, :piece]
        spaced = jnp.zeros((loops, 2, team, piece, rank), BF)
        spaced = lax.dynamic_update_slice(spaced, grad_down_in, (0, 0, seat, 0, 0))
        grad_down_enter = lax.psum_scatter(
            spaced.reshape(hidden_units, rank), "rows", scatter_dimension=0, tiled=True
        ).astype(F32)

    block_pos = place * seq_dev + jnp.arange(seq_dev, dtype=jnp.int32)
    valid = block_pos[None, :] < sizes_here[:, None]
    counts_here = jnp.sum(
        ((exit_depth[None] == levels[:, None, None]) & valid[None]).astype(F32), axis=(1, 2)
    )
    given = inputs.astype(F32)
    cross = jnp.sum(given * result, axis=-1)
    own_sq = jnp.sum(given * given, axis=-1)
    out_sq = jnp.sum(result * result, axis=-1)
    cosines = cross * lax.rsqrt(own_sq * out_sq + 1e-06)
    cosine_here = jnp.sum(jnp.where(positions < size_here, cosines, 0.0))
    tallies = jnp.concatenate([counts_here, cosine_here[None]])
    gain_grads = jnp.concatenate([grad_gain_first, grad_gain_second])
    gain_grads = gain_grads.reshape(2, loops * rows, gain_size).transpose(1, 0, 2)
    small = jnp.concatenate(
        [
            jnp.broadcast_to(tallies[None], (loops * rows, loops + 1)),
            gain_grads.reshape(loops * rows, 2 * gain_size),
        ],
        axis=1,
    )
    small = jnp.pad(small, ((0, 0), (0, 127 - loops - 2 * gain_size)))
    small = lax.all_to_all(small, ("depth", "rows"), split_axis=0, concat_axis=0, tiled=True)
    small = jnp.sum(small, axis=0)
    tallies = small[: loops + 1]
    gain_grads = small[loops + 1 : loops + 1 + 2 * gain_size].reshape(2, gain_size)
    exit_counts = tallies[:loops].astype(jnp.int32)
    confidence = tallies[loops] / jnp.sum(lengths).astype(F32)

    return (
        activations,
        grad_tokens,
        exit_counts,
        confidence,
        gain_grads[0],
        gain_grads[1],
        own_qkv,
        own_out,
        grad_gateup_weight,
        grad_down_weight,
        attn_grads[0][None],
        attn_grads[1][None],
        attn_grads[2][None],
        rest_grads[0][None],
        rest_grads[1][None],
        rest_grads[2][None],
        grad_gateup_leave[None],
        grad_down_enter[None],
        rest_grads[3][None],
    )


def solution(mesh):
    split = P("depth", "rows", None)
    flat = P(("depth", "rows"))
    tall = P(("depth", "rows"), None)
    return jax.shard_map(
        per_device,
        mesh=mesh,
        in_specs=(split, split, P("depth", "rows"), P(), P(), flat, flat)
        + (tall,) * 4
        + (split,) * 9,
        out_specs=(split, split, P(), P(), flat, flat) + (tall,) * 4 + (split,) * 9,
        check_vma=False,
    )
```

profile of v0, /device:TPU:0, one launch (start us, length us, event | category | flops | bytes accessed | tf_op | source)
XLA Modules:
  0.0 892.4 jit_solution(4989386246064430916)
XLA Ops:
  35.2 9.7 %collective-permute-done.2 = bf16[128,1152]{1,0:T(8,128)(2,1)S(1)} collective-permute-done((bf16[128,1152]{1,0:T(8,128)(2,1)}, bf16[128,1152]{1,0:T(8,128)(2,1)S(1)}, u32[]{:S(2)}, u32[]{:S(2)}) %collective-permute-start.2) | collective-permute-done | bytes 294944 | tf_op jit(solution)/shard_map/ppermute | solution.py:36
  44.9 41.0 %collective-permute-done.1 = bf16[128,1152]{1,0:T(8,128)(2,1)S(1)} collective-permute-done((bf16[128,1152]{1,0:T(8,128)(2,1)S(1)}, bf16[128,1152]{1,0:T(8,128)(2,1)S(1)}, u32[]{:S(2)}, u32[]{:S(2)}) %collective-permute-start.1) | collective-permute-done | bytes 294944 | tf_op jit(solution)/shard_map/ppermute | solution.py:36
  97.7 32.4 %collective-permute-done.5 = bf16[128,1152]{1,0:T(8,128)(2,1)S(1)} collective-permute-done((bf16[128,1152]{1,0:T(8,128)(2,1)S(1)}, bf16[128,1152]{1,0:T(8,128)(2,1)S(1)}, u32[]{:S(2)}, u32[]{:S(2)}) %collective-permute-start.5) | collective-permute-done | bytes 294944 | tf_op jit(solution)/shard_map/ppermute | solution.py:36
  133.2 12.4 %collective-permute-done.3 = bf16[128,1152]{1,0:T(8,128)(2,1)S(1)} collective-permute-done((bf16[128,1152]{1,0:T(8,128)(2,1)S(1)}, bf16[128,1152]{1,0:T(8,128)(2,1)S(1)}, u32[]{:S(2)}, u32[]{:S(2)}) %collective-permute-start.3) | collective-permute-done | bytes 294944 | tf_op jit(solution)/shard_map/ppermute | solution.py:36
  162.2 18.0 %collective-permute-done.9.refs_3_ = bf16[272,1536]{1,0:T(8,128)(2,1)S(1)} collective-permute-done((bf16[272,1536]{1,0:T(8,128)(2,1)S(1)}, bf16[272,1536]{1,0:T(8,128)(2,1)S(1)}, u32[]{:S(2)}, u32[]{:S(2)}) %collective-permute-start.9) | collective-permute-done | bytes 835616 | tf_op jit(solution)/shard_map/ppermute | solution.py:36
  180.2 18.3 %collective-permute-done.10.refs_5_ = bf16[272,1536]{1,0:T(8,128)(2,1)S(1)} collective-permute-done((bf16[272,1536]{1,0:T(8,128)(2,1)S(1)}, bf16[272,1536]{1,0:T(8,128)(2,1)S(1)}, u32[]{:S(2)}, u32[]{:S(2)}) %collective-permute-start.10) | collective-permute-done | bytes 835616 | tf_op jit(solution)/shard_map/ppermute | solution.py:36
  198.5 23.9 %collective-permute-done.12.refs_1_ = bf16[224,3584]{1,0:T(8,128)(2,1)} collective-permute-done((bf16[224,3584]{1,0:T(8,128)(2,1)}, bf16[224,3584]{1,0:T(8,128)(2,1)}, u32[]{:S(2)}, u32[]{:S(2)}) %collective-permute-start.12) | collective-permute-done | bytes 1605664 | tf_op jit(solution)/shard_map/ppermute | solution.py:36
  240.9 11.6 %shard_map.344 = (bf16[1152,1536]{1,0:T(8,128)(2,1)}, bf16[1024,1152]{1,0:T(8,128)(2,1)}) custom-call(s32[8]{0:T(128)} %stack.147.refs_0_, bf16[272,1536]{1,0:T(8,128)(2,1)} %copy-done.24, bf16[272,1536]{1,0:T(8,128)(2,1)} %fusion.19.refs_2_, bf16[272,1536]{1,0:T(8,128)(2,1)} %copy-done.21, bf16[272,1536]{1,0:T(8,128)(2,1)} %get-tuple-element.309.refs_4_, ...), custom_call_target="tpu_custom_call" | custom-call | tf_op jit(solution)/shard_map/pallas_call | solution.py:774
  252.5 5.8 shard_map.345
  258.3 6.4 collective-permute-done.16.refs_3_
  266.5 42.4 %collective-permute-done.14.refs_2_ = bf16[4,48,3584]{2,1,0:T(8,128)(2,1)} collective-permute-done((bf16[4,48,3584]{2,1,0:T(8,128)(2,1)}, bf16[4,48,3584]{2,1,0:T(8,128)(2,1)}, u32[]{:S(2)}, u32[]{:S(2)}) %collective-permute-start.14) | collective-permute-done | bytes 1376288 | tf_op jit(solution)/shard_map/ppermute | solution.py:36
  316.2 9.6 %shard_map.346 = (bf16[512,1024]{1,0:T(8,128)(2,1)}, f32[4,512,1]{2,1,0:T(8,128)}) custom-call(s32[1]{0:T(128)} %dynamic_slice.44.size_ref, bf16[512,1024]{1,0:T(8,128)(2,1)} %get-tuple-element.182.q_ref, bf16[1024,512]{1,0:T(8,128)(2,1)} %copy-done.14, s32[512,1]{1,0:T(8,128)} %copy.50.pos_ref, s32[1,1024]{1,0:T(1,128)} %bitcast.171), custom_call_target="tpu_custom_call" | custom-call | tf_op jit(solution)/shard_map/pallas_call | solution.py:304
  331.0 6.4 collective-permute-done.22
  337.4 8.9 collective-permute-done.20.refs_6_
  355.2 17.3 %shard_map.350 = (bf16[1152,3584]{1,0:T(8,128)(2,1)}, bf16[1792,1152]{1,0:T(8,128)(2,1)}) custom-call(s32[8]{0:T(128)} %stack.164.order_ref, bf16[224,3584]{1,0:T(8,128)(2,1)} %get-tuple-element.203.refs_0_, bf16[224,3584]{1,0:T(8,128)(2,1)} %collective-permute-done.12.refs_1_, bf16[224,3584]{1,0:T(8,128)(2,1)} %collective-permute-done.15.refs_2_, ...), custom_call_target="tpu_custom_call" | custom-call | tf_op jit(solution)/shard_map/pallas_call | solution.py:721
  386.3 60.6 %shard_map.351 = (bf16[2048,1792]{1,0:T(8,128)(2,1)}, bf16[2048,3584]{1,0:T(8,128)(2,1)}, bf16[2048,1152]{1,0:T(8,128)(2,1)}) custom-call(bf16[2048,1152]{1,0:T(8,128)(2,1)} %constant_dynamic-update-slice_fusion.2.n2_ref, bf16[2048,1152]{1,0:T(8,128)(2,1)} %constant_dynamic-update-slice_fusion.5.df_ref, bf16[1152,3584]{1,0:T(8,128)(2,1)} %get-tuple-element.219.wg_ref, ...), custom_call_target="tpu_custom_call" | custom-call | tf_op jit(solution)/shard_map/pallas_call | solution.py:534
  456.8 24.9 %convolution_convert_fusion.gateup_ref.refs_4_.refs_8_ = bf16[1152,3584]{1,0:T(8,128)(2,1)} fusion(bf16[2048,1152]{1,0:T(8,128)(2,1)} %constant_dynamic-update-slice_fusion.2.n2_ref, bf16[2048,3584]{1,0:T(8,128)(2,1)} %get-tuple-element.225), kind=kOutput, calls=%fused_computation.7 | convolution fusion | flops 16915562496 | bytes 27656192 | tf_op jit(solution)/shard_map/dot_general | solution.py:27
  481.6 14.1 %convolution_convert_fusion.1.down_ref.refs_5_.refs_6_.refs_10_ = bf16[1792,1152]{1,0:T(8,128)(2,1)} fusion(bf16[2048,1792]{1,0:T(8,128)(2,1)S(1)} %bitcast.176, bf16[2048,1152]{1,0:T(8,128)(2,1)} %constant_dynamic-update-slice_fusion.5.df_ref), kind=kOutput, calls=%fused_computation.8 | convolution fusion | flops 8457781248 | bytes 16187392 | tf_op jit(solution)/shard_map/dot_general | solution.py:27
  506.6 10.6 %shard_map.354 = (bf16[4,48,3584]{2,1,0:T(8,128)(2,1)}, bf16[4,48,3584]{2,1,0:T(8,128)(2,1)}) custom-call(s32[2]{0:T(128)} %pad_add_fusion.1.order_ref, bf16[1152,512]{1,0:T(8,128)(2,1)} %get-tuple-element.193.refs_8_.refs_0_.refs_1_.refs_2_.refs_3_, bf16[1152,512]{1,0:T(8,128)(2,1)} %get-tuple-element.193.refs_8_.refs_0_.refs_1_.refs_2_.refs_3_, ...), custom_call_target="tpu_custom_call" | custom-call | tf_op jit(solution)/shard_map/pallas_call | solution.py:885
  525.9 7.3 shard_map.355
  533.2 12.7 %shard_map.356 = (bf16[512,1024]{1,0:T(8,128)(2,1)}, bf16[1024,512]{1,0:T(8,128)(2,1)}) custom-call(s32[1]{0:T(128)} %dynamic_slice.44.size_ref, bf16[512,1024]{1,0:T(8,128)(2,1)} %get-tuple-element.182.q_ref, bf16[1024,512]{1,0:T(8,128)(2,1)} %copy-done.14, bf16[512,1024]{1,0:T(8,128)(2,1)} %get-tuple-element.238.do_ref, ...), custom_call_target="tpu_custom_call" | custom-call | tf_op jit(solution)/shard_map/pallas_call | solution.py:366
  545.8 11.9 %convolution_convert_fusion.3 = bf16[2048,1152]{1,0:T(8,128)(2,1)S(1)} fusion(bf16[2048,1792]{1,0:T(8,128)(2,1)} %get-tuple-element.244, bf16[1792,1152]{1,0:T(8,128)(2,1)S(1)} %copy-done.20), kind=kOutput, calls=%fused_computation.10 | convolution fusion | flops 8458076160 | bytes 16187392 | tf_op jit(solution)/shard_map/dot_general | solution.py:23
  557.7 29.4 %collective-permute-done.30.refs_3_ = bf16[4,48,3584]{2,1,0:T(8,128)(2,1)} collective-permute-done((bf16[4,48,3584]{2,1,0:T(8,128)(2,1)}, bf16[4,48,3584]{2,1,0:T(8,128)(2,1)}, u32[]{:S(2)}, u32[]{:S(2)}) %collective-permute-start.30) | collective-permute-done | bytes 1376288 | tf_op jit(solution)/shard_map/ppermute | solution.py:36
  605.3 7.6 shard_map.359
  616.9 12.4 %collective-permute-done.31 = bf16[224,3584]{1,0:T(8,128)(2,1)} collective-permute-done((bf16[224,3584]{1,0:T(8,128)(2,1)}, bf16[224,3584]{1,0:T(8,128)(2,1)}, u32[]{:S(2)}, u32[]{:S(2)}) %collective-permute-start.31) | collective-permute-done | bytes 1605664 | tf_op jit(solution)/shard_map/ppermute | solution.py:36
  648.8 57.4 %collective-permute-done.36.refs_1_ = bf16[224,3584]{1,0:T(8,128)(2,1)S(1)} collective-permute-done((bf16[224,3584]{1,0:T(8,128)(2,1)S(1)}, bf16[224,3584]{1,0:T(8,128)(2,1)S(1)}, u32[]{:S(2)}, u32[]{:S(2)}) %collective-permute-start.36) | collective-permute-done | bytes 1605664 | tf_op jit(solution)/shard_map/ppermute | solution.py:36
  711.5 15.5 %shard_map.363 = bf16[8,896,256]{2,1,0:T(8,128)(2,1)} custom-call(s32[8]{0:T(128)} %iota.55.refs_0_, bf16[544,1536]{1,0:T(8,128)(2,1)} %fusion.8.refs_1_, bf16[544,1536]{1,0:T(8,128)(2,1)} %copy-done.12, bf16[544,1536]{1,0:T(8,128)(2,1)} %copy-done.13, bf16[544,1536]{1,0:T(8,128)(2,1)} %collective-permute-done.39.refs_4_, ...), custom_call_target="tpu_custom_call" | custom-call | tf_op jit(solution)/shard_map/pallas_call | solution.py:192
  727.9 9.8 %shard_map.361 = bf16[8,912,256]{2,1,0:T(8,128)(2,1)} custom-call(s32[8]{0:T(128)} %iota.54.refs_0_, bf16[544,1536]{1,0:T(8,128)(2,1)} %fusion.8.refs_1_, bf16[544,1536]{1,0:T(8,128)(2,1)} %copy-done.12, bf16[544,1536]{1,0:T(8,128)(2,1)} %copy-done.13, bf16[544,1536]{1,0:T(8,128)(2,1)} %collective-permute-done.39.refs_4_, bf16[1152,1536]{1,0:T(8,128)(2,1)} %copy-done.4, ...), custom_call_target="tpu_custom_call" | custom-call | tf_op jit(solution)/shard_map/pallas_call | solution.py:192
  759.2 51.3 %collective-permute-done.42 = bf16[256,1152]{1,0:T(8,128)(2,1)} collective-permute-done((bf16[256,1152]{1,0:T(8,128)(2,1)}, bf16[256,1152]{1,0:T(8,128)(2,1)}, u32[]{:S(2)}, u32[]{:S(2)}) %collective-permute-start.42) | collective-permute-done | bytes 589856 | tf_op jit(solution)/shard_map/ppermute | solution.py:36
  810.5 8.5 collective-permute-done.41
  818.9 24.9 %collective-permute-done.40 = bf16[256,1152]{1,0:T(8,128)(2,1)} collective-permute-done((bf16[256,1152]{1,0:T(8,128)(2,1)}, bf16[256,1152]{1,0:T(8,128)(2,1)}, u32[]{:S(2)}, u32[]{:S(2)}) %collective-permute-start.40) | collective-permute-done | bytes 589856 | tf_op jit(solution)/shard_map/ppermute | solution.py:36
  870.3 6.1 shard_map.365
  (308 shorter events, 246.3 us)
Async XLA Ops:
  7.2 139.6 %all-gather.3.cloned.1.call-start = ((), (), s32[]{:S(2)}) async-start(), calls=%async_computation.7 | async-start | bytes 6340608 | tf_op jit(solution)/shard_map/all_gather | solution.py:1081
  21.8 65.9 %all-to-all-start = ((bf16[4,128,1152]{2,1,0:T(8,128)(2,1)}), bf16[4,128,1152]{2,1,0:T(8,128)(2,1)S(1)}, u32[]{:S(2)}, u32[]{:S(2)}) async-start(bf16[4,128,1152]{2,1,0:T(8,128)(2,1)} %gather_fusion), calls=%async_computation | async-start | bytes 2359296 | tf_op jit(solution)/shard_map/all_to_all | solution.py:1082
  30.6 55.3 %collective-permute-start.1 = (bf16[128,1152]{1,0:T(8,128)(2,1)S(1)}, bf16[128,1152]{1,0:T(8,128)(2,1)S(1)}, u32[]{:S(2)}, u32[]{:S(2)}) collective-permute-start(bf16[128,1152]{1,0:T(8,128)(2,1)S(1)} %get-tuple-element.329), channel_id=1, source_target_pairs={{0,4},{1,5},{2,6},{3,7},{4,0},{5,1},{6,2},{7,3},{8,12},{9,13},{10,... | collective-permute-start | bytes 884744 | tf_op jit(solution)/shard_map/ppermute | solution.py:36
  30.6 55.3 %collective-permute-start = (bf16[128,1152]{1,0:T(8,128)(2,1)S(1)}, bf16[128,1152]{1,0:T(8,128)(2,1)S(1)}, u32[]{:S(2)}, u32[]{:S(2)}) collective-permute-start(bf16[128,1152]{1,0:T(8,128)(2,1)S(1)} %get-tuple-element.330), channel_id=1, source_target_pairs={{0,2},{1,3},{2,0},{3,1},{4,6},{5,7},{6,4},{7,5},{8,10},{9,11},{10,... | collective-permute-start | bytes 884744 | tf_op jit(solution)/shard_map/ppermute | solution.py:36
  87.7 59.1 %all-to-all-start.1 = ((bf16[4,84,3584]{2,1,0:T(8,128)(2,1)}), bf16[4,84,3584]{2,1,0:T(8,128)(2,1)}, u32[]{:S(2)}, u32[]{:S(2)}) async-start(bf16[4,84,3584]{2,1,0:T(8,128)(2,1)} %shard_map.339), calls=%async_computation.1 | async-start | bytes 5046272 | tf_op jit(solution)/shard_map/all_to_all | solution.py:1022
  92.3 258.6 %all-gather.5.cloned.1.call-start = ((), (), s32[]{:S(2)}) async-start(), calls=%async_computation.8 | async-start | bytes 2064384 | tf_op jit(solution)/shard_map/all_gather | solution.py:1122
  95.8 37.5 %collective-permute-start.4 = (bf16[128,1152]{1,0:T(8,128)(2,1)S(1)}, bf16[128,1152]{1,0:T(8,128)(2,1)S(1)}, u32[]{:S(2)}, u32[]{:S(2)}) collective-permute-start(bf16[128,1152]{1,0:T(8,128)(2,1)S(1)} %get-tuple-element.325), channel_id=1, source_target_pairs={{0,4},{1,5},{2,6},{3,7},{4,0},{5,1},{6,2},{7,3},{8,12},{9,13},{10,... | collective-permute-start | bytes 884744 | tf_op jit(solution)/shard_map/ppermute | solution.py:36
  96.6 49.0 %collective-permute-start.3 = (bf16[128,1152]{1,0:T(8,128)(2,1)S(1)}, bf16[128,1152]{1,0:T(8,128)(2,1)S(1)}, u32[]{:S(2)}, u32[]{:S(2)}) collective-permute-start(bf16[128,1152]{1,0:T(8,128)(2,1)S(1)} %get-tuple-element.326), channel_id=1, source_target_pairs={{0,2},{1,3},{2,0},{3,1},{4,6},{5,7},{6,4},{7,5},{8,10},{9,11},{10,... | collective-permute-start | bytes 884744 | tf_op jit(solution)/shard_map/ppermute | solution.py:36
  150.4 71.9 %collective-permute-start.12 = (bf16[224,3584]{1,0:T(8,128)(2,1)}, bf16[224,3584]{1,0:T(8,128)(2,1)}, u32[]{:S(2)}, u32[]{:S(2)}) collective-permute-start(bf16[224,3584]{1,0:T(8,128)(2,1)} %get-tuple-element.203.refs_0_), channel_id=1, source_target_pairs={{0,4},{1,5},{2,6},{3,7},{4,0},{5,1},{6,2},{7,3},{8,12},{9,13},{10,... | collective-permute-start | bytes 4816904 | tf_op jit(solution)/shard_map/ppermute | solution.py:36
  160.4 38.1 %collective-permute-start.10 = (bf16[272,1536]{1,0:T(8,128)(2,1)S(1)}, bf16[272,1536]{1,0:T(8,128)(2,1)S(1)}, u32[]{:S(2)}, u32[]{:S(2)}) collective-permute-start(bf16[272,1536]{1,0:T(8,128)(2,1)S(1)} %fusion.18.refs_1_), channel_id=1, source_target_pairs={{0,16},{8,24},{16,0},{24,8},{1,17},{9,25},{17,1},{25,9},{2,18},{10... | collective-permute-start | bytes 2506760 | tf_op jit(solution)/shard_map/ppermute | solution.py:36
  226.6 38.1 %collective-permute-start.16 = (bf16[224,3584]{1,0:T(8,128)(2,1)}, bf16[224,3584]{1,0:T(8,128)(2,1)S(1)}, u32[]{:S(2)}, u32[]{:S(2)}) collective-permute-start(bf16[224,3584]{1,0:T(8,128)(2,1)} %collective-permute-done.12.refs_1_), channel_id=1, source_target_pairs={{0,8},{8,0},{16,24},{24,16},{1,9},{9,1},{17,25},{25,17},{2,10},{10... | collective-permute-start | bytes 4816904 | tf_op jit(solution)/shard_map/ppermute | solution.py:36
  228.2 38.3 %collective-permute-start.18 = (bf16[224,3584]{1,0:T(8,128)(2,1)}, bf16[224,3584]{1,0:T(8,128)(2,1)}, u32[]{:S(2)}, u32[]{:S(2)}) collective-permute-start(bf16[224,3584]{1,0:T(8,128)(2,1)} %collective-permute-done.12.refs_1_), channel_id=1, source_target_pairs={{0,16},{8,24},{16,0},{24,8},{1,17},{9,25},{17,1},{25,9},{2,18},{10... | collective-permute-start | bytes 4816904 | tf_op jit(solution)/shard_map/ppermute | solution.py:36
  229.7 79.2 %collective-permute-start.15 = (bf16[224,3584]{1,0:T(8,128)(2,1)}, bf16[224,3584]{1,0:T(8,128)(2,1)}, u32[]{:S(2)}, u32[]{:S(2)}) collective-permute-start(bf16[224,3584]{1,0:T(8,128)(2,1)} %get-tuple-element.203.refs_0_), channel_id=1, source_target_pairs={{0,8},{8,0},{16,24},{24,16},{1,9},{9,1},{17,25},{25,17},{2,10},{10... | collective-permute-start | bytes 4816904 | tf_op jit(solution)/shard_map/ppermute | solution.py:36
  231.0 77.9 %collective-permute-start.17 = (bf16[224,3584]{1,0:T(8,128)(2,1)}, bf16[224,3584]{1,0:T(8,128)(2,1)}, u32[]{:S(2)}, u32[]{:S(2)}) collective-permute-start(bf16[224,3584]{1,0:T(8,128)(2,1)} %get-tuple-element.203.refs_0_), channel_id=1, source_target_pairs={{0,16},{8,24},{16,0},{24,8},{1,17},{9,25},{17,1},{25,9},{2,18},{10... | collective-permute-start | bytes 4816904 | tf_op jit(solution)/shard_map/ppermute | solution.py:36
  232.5 76.4 %collective-permute-start.14 = (bf16[4,48,3584]{2,1,0:T(8,128)(2,1)}, bf16[4,48,3584]{2,1,0:T(8,128)(2,1)}, u32[]{:S(2)}, u32[]{:S(2)}) collective-permute-start(bf16[4,48,3584]{2,1,0:T(8,128)(2,1)} %get-tuple-element.184.refs_1_), channel_id=1, source_target_pairs={{0,4},{1,5},{2,6},{3,7},{4,0},{5,1},{6,2},{7,3},{8,12},{9,13},{10,... | collective-permute-start | bytes 4128776 | tf_op jit(solution)/shard_map/ppermute | solution.py:36
  235.2 645.4 %reduce-scatter.5.cloned.1.call-start = ((), (), s32[]{:S(2)}) async-start(), calls=%async_computation.10 | async-start | bytes 4128768 | tf_op jit(solution)/shard_map/reduce_scatter | solution.py:1287
  308.9 37.3 %collective-permute-start.20 = (bf16[224,3584]{1,0:T(8,128)(2,1)}, bf16[224,3584]{1,0:T(8,128)(2,1)}, u32[]{:S(2)}, u32[]{:S(2)}) collective-permute-start(bf16[224,3584]{1,0:T(8,128)(2,1)} %collective-permute-done.15.refs_2_), channel_id=1, source_target_pairs={{0,16},{8,24},{16,0},{24,8},{1,17},{9,25},{17,1},{25,9},{2,18},{10... | collective-permute-start | bytes 4816904 | tf_op jit(solution)/shard_map/ppermute | solution.py:36
  309.5 37.1 %collective-permute-start.21 = (bf16[224,3584]{1,0:T(8,128)(2,1)}, bf16[224,3584]{1,0:T(8,128)(2,1)}, u32[]{:S(2)}, u32[]{:S(2)}) collective-permute-start(bf16[224,3584]{1,0:T(8,128)(2,1)} %collective-permute-done.18.refs_5_), channel_id=1, source_target_pairs={{0,8},{8,0},{16,24},{24,16},{1,9},{9,1},{17,25},{25,17},{2,10},{10... | collective-permute-start | bytes 4816904 | tf_op jit(solution)/shard_map/ppermute | solution.py:36
  455.4 40.4 %collective-permute-start.27 = (bf16[512,1152]{1,0:T(8,128)(2,1)S(1)}, bf16[512,1152]{1,0:T(8,128)(2,1)S(1)}, u32[]{:S(2)}, u32[]{:S(2)}) collective-permute-start(bf16[512,1152]{1,0:T(8,128)(2,1)S(1)} %get-tuple-element.322), channel_id=1, source_target_pairs={{0,2},{1,3},{2,0},{3,1},{4,6},{5,7},{6,4},{7,5},{8,10},{9,11},{10,... | collective-permute-start | bytes 3538952 | tf_op jit(solution)/shard_map/ppermute | solution.py:36
  503.5 83.6 %collective-permute-start.28 = (bf16[2,224,3584]{2,1,0:T(8,128)(2,1)}, bf16[2,224,3584]{2,1,0:T(8,128)(2,1)}, u32[]{:S(2)}, u32[]{:S(2)}) collective-permute-start(bf16[2,224,3584]{2,1,0:T(8,128)(2,1)} %shard_map.352), channel_id=1, source_target_pairs={{0,16},{8,24},{16,0},{24,8},{1,17},{9,25},{17,1},{25,9},{2,18},{10... | collective-permute-start | bytes 9633800 | tf_op jit(solution)/shard_map/ppermute | solution.py:36
  504.9 82.2 %collective-permute-start.29 = (bf16[2,224,3584]{2,1,0:T(8,128)(2,1)}, bf16[2,224,3584]{2,1,0:T(8,128)(2,1)}, u32[]{:S(2)}, u32[]{:S(2)}) collective-permute-start(bf16[2,224,3584]{2,1,0:T(8,128)(2,1)} %shard_map.353), channel_id=1, source_target_pairs={{0,8},{8,0},{16,24},{24,16},{1,9},{9,1},{17,25},{25,17},{2,10},{10... | collective-permute-start | bytes 9633800 | tf_op jit(solution)/shard_map/ppermute | solution.py:36
  525.0 62.1 %collective-permute-start.30 = (bf16[4,48,3584]{2,1,0:T(8,128)(2,1)}, bf16[4,48,3584]{2,1,0:T(8,128)(2,1)}, u32[]{:S(2)}, u32[]{:S(2)}) collective-permute-start(bf16[4,48,3584]{2,1,0:T(8,128)(2,1)} %get-tuple-element.245), channel_id=1, source_target_pairs={{0,4},{1,5},{2,6},{3,7},{4,0},{5,1},{6,2},{7,3},{8,12},{9,13},{10,... | collective-permute-start | bytes 4128776 | tf_op jit(solution)/shard_map/ppermute | solution.py:36
  592.1 37.3 %collective-permute-start.31 = (bf16[224,3584]{1,0:T(8,128)(2,1)}, bf16[224,3584]{1,0:T(8,128)(2,1)}, u32[]{:S(2)}, u32[]{:S(2)}) collective-permute-start(bf16[224,3584]{1,0:T(8,128)(2,1)} %fusion.14), channel_id=1, source_target_pairs={{0,8},{8,0},{16,24},{24,16},{1,9},{9,1},{17,25},{25,17},{2,10},{10... | collective-permute-start | bytes 4816904 | tf_op jit(solution)/shard_map/ppermute | solution.py:36
  636.0 70.2 %collective-permute-start.36 = (bf16[224,3584]{1,0:T(8,128)(2,1)S(1)}, bf16[224,3584]{1,0:T(8,128)(2,1)S(1)}, u32[]{:S(2)}, u32[]{:S(2)}) collective-permute-start(bf16[224,3584]{1,0:T(8,128)(2,1)S(1)} %fusion.4), channel_id=1, source_target_pairs={{0,4},{1,5},{2,6},{3,7},{4,0},{5,1},{6,2},{7,3},{8,12},{9,13},{10,... | collective-permute-start | bytes 4816904 | tf_op jit(solution)/shard_map/ppermute | solution.py:36
  636.7 69.6 %collective-permute-start.37 = (bf16[544,1536]{1,0:T(8,128)(2,1)S(1)}, bf16[544,1536]{1,0:T(8,128)(2,1)S(1)}, u32[]{:S(2)}, u32[]{:S(2)}) collective-permute-start(bf16[544,1536]{1,0:T(8,128)(2,1)S(1)} %fusion.9), channel_id=1, source_target_pairs={{0,8},{8,0},{16,24},{24,16},{1,9},{9,1},{17,25},{25,17},{2,10},{10... | collective-permute-start | bytes 5013512 | tf_op jit(solution)/shard_map/ppermute | solution.py:36
  637.5 72.8 %collective-permute-start.38 = (bf16[544,1536]{1,0:T(8,128)(2,1)S(1)}, bf16[544,1536]{1,0:T(8,128)(2,1)S(1)}, u32[]{:S(2)}, u32[]{:S(2)}) collective-permute-start(bf16[544,1536]{1,0:T(8,128)(2,1)S(1)} %fusion.10), channel_id=1, source_target_pairs={{0,16},{8,24},{16,0},{24,8},{1,17},{9,25},{17,1},{25,9},{2,18},{10... | collective-permute-start | bytes 5013512 | tf_op jit(solution)/shard_map/ppermute | solution.py:36
  638.0 72.3 %collective-permute-start.39 = (bf16[544,1536]{1,0:T(8,128)(2,1)S(1)}, bf16[544,1536]{1,0:T(8,128)(2,1)}, u32[]{:S(2)}, u32[]{:S(2)}) collective-permute-start(bf16[544,1536]{1,0:T(8,128)(2,1)S(1)} %fusion.11), channel_id=1, source_target_pairs={{0,24},{8,16},{16,8},{24,0},{1,25},{9,17},{17,9},{25,1},{2,26},{10... | collective-permute-start | bytes 5013512 | tf_op jit(solution)/shard_map/ppermute | solution.py:36
  727.0 155.5 %reduce-scatter.3.cloned.1.call-start = ((), (), s32[]{:S(2)}) async-start(), calls=%async_computation.9 | async-start | bytes 4202496 | tf_op jit(solution)/shard_map/reduce_scatter | solution.py:1287
  744.7 102.4 %all-to-all-start.2 = ((bf16[4,84,3584]{2,1,0:T(8,128)(2,1)}), bf16[4,84,3584]{2,1,0:T(8,128)(2,1)S(1)}, u32[]{:S(2)}, u32[]{:S(2)}) async-start(bf16[4,84,3584]{2,1,0:T(8,128)(2,1)} %get-tuple-element.275), calls=%async_computation.2 | async-start | bytes 5046272 | tf_op jit(solution)/shard_map/all_to_all | solution.py:1022
  751.7 58.8 %collective-permute-start.42 = (bf16[256,1152]{1,0:T(8,128)(2,1)}, bf16[256,1152]{1,0:T(8,128)(2,1)}, u32[]{:S(2)}, u32[]{:S(2)}) collective-permute-start(bf16[256,1152]{1,0:T(8,128)(2,1)} %get-tuple-element.313), channel_id=1, source_target_pairs={{0,6},{1,7},{2,4},{3,5},{4,2},{5,3},{6,0},{7,1},{8,14},{9,15},{10,... | collective-permute-start | bytes 1769480 | tf_op jit(solution)/shard_map/ppermute | solution.py:36
  755.7 63.3 %collective-permute-start.41 = (bf16[256,1152]{1,0:T(8,128)(2,1)}, bf16[256,1152]{1,0:T(8,128)(2,1)}, u32[]{:S(2)}, u32[]{:S(2)}) collective-permute-start(bf16[256,1152]{1,0:T(8,128)(2,1)} %get-tuple-element.314), channel_id=1, source_target_pairs={{0,4},{1,5},{2,6},{3,7},{4,0},{5,1},{6,2},{7,3},{8,12},{9,13},{10,... | collective-permute-start | bytes 1769480 | tf_op jit(solution)/shard_map/ppermute | solution.py:36
  755.7 88.2 %collective-permute-start.40 = (bf16[256,1152]{1,0:T(8,128)(2,1)}, bf16[256,1152]{1,0:T(8,128)(2,1)}, u32[]{:S(2)}, u32[]{:S(2)}) collective-permute-start(bf16[256,1152]{1,0:T(8,128)(2,1)} %get-tuple-element.315), channel_id=1, source_target_pairs={{0,2},{1,3},{2,0},{3,1},{4,6},{5,7},{6,4},{7,5},{8,10},{9,11},{10,... | collective-permute-start | bytes 1769480 | tf_op jit(solution)/shard_map/ppermute | solution.py:36
  (69 other events, 1543.6 us)
Sparse Core Ops, SparseCore 0:
  19.3 84.0 all-gather.2
  235.3 52.9 all-gather.4
  727.2 60.4 reduce-scatter.4
  789.8 81.9 reduce-scatter.2
where the time goes:
time: 900 us; the launch traced here: 892 us
  waiting for transfers between devices  428 us (48%)
  Pallas kernels  227 us (25%)
  starting transfers between devices  61.1 us (7%)
  matrix products  57.8 us (6%)
  local copies, waits for them, and re-layouts  56.9 us (6%)
  other arithmetic  44.6 us (5%)
  between operations  17.1 us (2%)
    ppermute x43, waiting for transfers between devices, swap(): return lax.ppermute(value, axis, [(i, i ^ flip) for i in range(size)])  425 us
    pallas_call x1, Pallas kernels, ff_pass(): pl.pallas_call(ff_kernel, grid=(count // tile,), in_specs=[strip(tile, wi...  60.6 us
    dot_general x4, matrix products, outer_sum(): lax.dot_general(left, right, (((0,), (0,)), ((), ())), preferred_element_...  46 us
    ppermute x43, starting transfers between devices, swap(): return lax.ppermute(value, axis, [(i, i ^ flip) for i in range(size)])  39.3 us
    pallas_call x2, Pallas kernels, grads_pass(): pl.pallas_call(kernel, in_specs=[pl.BlockSpec(memory_space=pltpu.SMEM)] +...  25.4 us
  transfers between devices with their start and end apart: 52, of which 29 were waited for; matrix products, arithmetic and copies ran while one was open for 16% of the time, Pallas kernels for 15%

commit v1 on v0

--- a/solution.py
+++ b/solution.py
@@ -1178,8 +1178,10 @@
         full_down_leave,
         padded,
     )
-    normed_far, gateup_eff, down_eff = tie(normed_far, gateup_eff, down_eff)
     cotan_team = gather_team(upstream_low, cotan_far)
+    normed_far, gateup_eff, down_eff, cotan_team = tie(
+        normed_far, gateup_eff, down_eff, cotan_team
+    )
     normed_team = gather_team(normed_two, normed_far)
 
     hidden, grad_expanded, grad_normed = ff_pass(

time: 900 us -> 896 us (level)
  transfers between devices with their start and end apart: 52 -> 52, of which waited for: 29 -> 28; matrix products, arithmetic and copies ran while one was open for 16% -> 15% of each run, Pallas kernels for 15% -> 15%
where the time goes in v1:
time: 896 us; the launch traced here: 887 us
  waiting for transfers between devices  424 us (47%)
  Pallas kernels  226 us (25%)
  starting transfers between devices  62 us (7%)
  matrix products  55.8 us (6%)
  local copies, waits for them, and re-layouts  53.6 us (6%)
  other arithmetic  48.4 us (5%)
  between operations  17.3 us (2%)
    ppermute x43, waiting for transfers between devices, swap(): return lax.ppermute(value, axis, [(i, i ^ flip) for i in range(size)])  421 us
    pallas_call x1, Pallas kernels, ff_pass(): pl.pallas_call(ff_kernel, grid=(count // tile,), in_specs=[strip(tile, wi...  60.5 us
    dot_general x4, matrix products, outer_sum(): lax.dot_general(left, right, (((0,), (0,)), ((), ())), preferred_element_...  43.9 us
    ppermute x43, starting transfers between devices, swap(): return lax.ppermute(value, axis, [(i, i ^ flip) for i in range(size)])  40.5 us
    pallas_call x2, Pallas kernels, grads_pass(): pl.pallas_call(kernel, in_specs=[pl.BlockSpec(memory_space=pltpu.SMEM)] +...  25.3 us
  transfers between devices with their start and end apart: 52, of which 28 were waited for; matrix products, arithmetic and copies ran while one was open for 15% of the time, Pallas kernels for 15%

profile of v1, /device:TPU:0, one launch (start us, length us, event | category | flops | bytes accessed | tf_op | source)
XLA Modules:
  0.0 887.4 jit_solution(9516067945964486261)
XLA Ops:
  35.2 9.7 %collective-permute-done.2 = bf16[128,1152]{1,0:T(8,128)(2,1)S(1)} collective-permute-done((bf16[128,1152]{1,0:T(8,128)(2,1)}, bf16[128,1152]{1,0:T(8,128)(2,1)S(1)}, u32[]{:S(2)}, u32[]{:S(2)}) %collective-permute-start.2) | collective-permute-done | bytes 294944 | tf_op jit(solution)/shard_map/ppermute | solution.py:36
  44.9 41.0 %collective-permute-done.1 = bf16[128,1152]{1,0:T(8,128)(2,1)S(1)} collective-permute-done((bf16[128,1152]{1,0:T(8,128)(2,1)S(1)}, bf16[128,1152]{1,0:T(8,128)(2,1)S(1)}, u32[]{:S(2)}, u32[]{:S(2)}) %collective-permute-start.1) | collective-permute-done | bytes 294944 | tf_op jit(solution)/shard_map/ppermute | solution.py:36
  97.7 32.4 %collective-permute-done.5 = bf16[128,1152]{1,0:T(8,128)(2,1)S(1)} collective-permute-done((bf16[128,1152]{1,0:T(8,128)(2,1)S(1)}, bf16[128,1152]{1,0:T(8,128)(2,1)S(1)}, u32[]{:S(2)}, u32[]{:S(2)}) %collective-permute-start.5) | collective-permute-done | bytes 294944 | tf_op jit(solution)/shard_map/ppermute | solution.py:36
  133.2 12.4 %collective-permute-done.3 = bf16[128,1152]{1,0:T(8,128)(2,1)S(1)} collective-permute-done((bf16[128,1152]{1,0:T(8,128)(2,1)S(1)}, bf16[128,1152]{1,0:T(8,128)(2,1)S(1)}, u32[]{:S(2)}, u32[]{:S(2)}) %collective-permute-start.3) | collective-permute-done | bytes 294944 | tf_op jit(solution)/shard_map/ppermute | solution.py:36
  162.2 18.0 %collective-permute-done.9.refs_3_ = bf16[272,1536]{1,0:T(8,128)(2,1)S(1)} collective-permute-done((bf16[272,1536]{1,0:T(8,128)(2,1)S(1)}, bf16[272,1536]{1,0:T(8,128)(2,1)S(1)}, u32[]{:S(2)}, u32[]{:S(2)}) %collective-permute-start.9) | collective-permute-done | bytes 835616 | tf_op jit(solution)/shard_map/ppermute | solution.py:36
  180.2 18.3 %collective-permute-done.10.refs_5_ = bf16[272,1536]{1,0:T(8,128)(2,1)S(1)} collective-permute-done((bf16[272,1536]{1,0:T(8,128)(2,1)S(1)}, bf16[272,1536]{1,0:T(8,128)(2,1)S(1)}, u32[]{:S(2)}, u32[]{:S(2)}) %collective-permute-start.10) | collective-permute-done | bytes 835616 | tf_op jit(solution)/shard_map/ppermute | solution.py:36
  198.5 23.9 %collective-permute-done.12.refs_1_ = bf16[224,3584]{1,0:T(8,128)(2,1)} collective-permute-done((bf16[224,3584]{1,0:T(8,128)(2,1)}, bf16[224,3584]{1,0:T(8,128)(2,1)}, u32[]{:S(2)}, u32[]{:S(2)}) %collective-permute-start.12) | collective-permute-done | bytes 1605664 | tf_op jit(solution)/shard_map/ppermute | solution.py:36
  240.2 11.5 %shard_map.344 = (bf16[1152,1536]{1,0:T(8,128)(2,1)}, bf16[1024,1152]{1,0:T(8,128)(2,1)}) custom-call(s32[8]{0:T(128)} %stack.147.refs_0_, bf16[272,1536]{1,0:T(8,128)(2,1)} %copy-done.23, bf16[272,1536]{1,0:T(8,128)(2,1)} %fusion.19.refs_2_, bf16[272,1536]{1,0:T(8,128)(2,1)} %copy-done.20, bf16[272,1536]{1,0:T(8,128)(2,1)} %get-tuple-element.311.refs_4_, ...), custom_call_target="tpu_custom_call" | custom-call | tf_op jit(solution)/shard_map/pallas_call | solution.py:774
  251.7 5.7 shard_map.345
  257.4 7.2 collective-permute-done.16.refs_3_
  266.5 27.7 %collective-permute-done.14.refs_2_ = bf16[4,48,3584]{2,1,0:T(8,128)(2,1)} collective-permute-done((bf16[4,48,3584]{2,1,0:T(8,128)(2,1)}, bf16[4,48,3584]{2,1,0:T(8,128)(2,1)}, u32[]{:S(2)}, u32[]{:S(2)}) %collective-permute-start.14) | collective-permute-done | bytes 1376288 | tf_op jit(solution)/shard_map/ppermute | solution.py:36
  308.7 9.6 %shard_map.346 = (bf16[512,1024]{1,0:T(8,128)(2,1)}, f32[4,512,1]{2,1,0:T(8,128)}) custom-call(s32[1]{0:T(128)} %dynamic_slice.44.size_ref, bf16[512,1024]{1,0:T(8,128)(2,1)} %get-tuple-element.183.q_ref, bf16[1024,512]{1,0:T(8,128)(2,1)} %copy-done.14, s32[512,1]{1,0:T(8,128)} %copy.50.pos_ref, s32[1,1024]{1,0:T(1,128)} %bitcast.173), custom_call_target="tpu_custom_call" | custom-call | tf_op jit(solution)/shard_map/pallas_call | solution.py:304
  323.5 20.2 %collective-permute-done.22 = bf16[512,1152]{1,0:T(8,128)(2,1)S(1)} collective-permute-done((bf16[512,1152]{1,0:T(8,128)(2,1)S(1)}, bf16[512,1152]{1,0:T(8,128)(2,1)S(1)}, u32[]{:S(2)}, u32[]{:S(2)}) %collective-permute-start.22) | collective-permute-done | bytes 1179680 | tf_op jit(solution)/shard_map/ppermute | solution.py:36
  352.5 17.4 %shard_map.350 = (bf16[1152,3584]{1,0:T(8,128)(2,1)}, bf16[1792,1152]{1,0:T(8,128)(2,1)}) custom-call(s32[8]{0:T(128)} %stack.164.order_ref, bf16[224,3584]{1,0:T(8,128)(2,1)} %get-tuple-element.204.refs_0_, bf16[224,3584]{1,0:T(8,128)(2,1)} %collective-permute-done.12.refs_1_, bf16[224,3584]{1,0:T(8,128)(2,1)} %collective-permute-done.15.refs_2_, ...), custom_call_target="tpu_custom_call" | custom-call | tf_op jit(solution)/shard_map/pallas_call | solution.py:721
  382.5 60.5 %shard_map.351 = (bf16[2048,1792]{1,0:T(8,128)(2,1)}, bf16[2048,3584]{1,0:T(8,128)(2,1)}, bf16[2048,1152]{1,0:T(8,128)(2,1)}) custom-call(bf16[2048,1152]{1,0:T(8,128)(2,1)} %constant_dynamic-update-slice_fusion.2.n2_ref, bf16[2048,1152]{1,0:T(8,128)(2,1)} %pad_maximum_fusion.df_ref, bf16[1152,3584]{1,0:T(8,128)(2,1)} %get-tuple-element.221.wg_ref, ...), custom_call_target="tpu_custom_call" | custom-call | tf_op jit(solution)/shard_map/pallas_call | solution.py:534
  453.2 25.0 %convolution_convert_fusion.gateup_ref.refs_4_.refs_8_ = bf16[1152,3584]{1,0:T(8,128)(2,1)} fusion(bf16[2048,1152]{1,0:T(8,128)(2,1)} %constant_dynamic-update-slice_fusion.2.n2_ref, bf16[2048,3584]{1,0:T(8,128)(2,1)} %get-tuple-element.227), kind=kOutput, calls=%fused_computation.7 | convolution fusion | flops 16915562496 | bytes 27656192 | tf_op jit(solution)/shard_map/dot_general | solution.py:27
  478.3 11.9 %convolution_convert_fusion.1.down_ref.refs_5_.refs_6_.refs_10_ = bf16[1792,1152]{1,0:T(8,128)(2,1)} fusion(bf16[2048,1792]{1,0:T(8,128)(2,1)S(1)} %bitcast.178, bf16[2048,1152]{1,0:T(8,128)(2,1)S(1)} %bitcast.151), kind=kOutput, calls=%fused_computation.8 | convolution fusion | flops 8457781248 | bytes 16187392 | tf_op jit(solution)/shard_map/dot_general | solution.py:27
  501.1 10.6 %shard_map.354 = (bf16[4,48,3584]{2,1,0:T(8,128)(2,1)}, bf16[4,48,3584]{2,1,0:T(8,128)(2,1)}) custom-call(s32[2]{0:T(128)} %pad_add_fusion.1.order_ref, bf16[1152,512]{1,0:T(8,128)(2,1)} %get-tuple-element.194.refs_8_.refs_0_.refs_1_.refs_2_.refs_3_, bf16[1152,512]{1,0:T(8,128)(2,1)} %get-tuple-element.194.refs_8_.refs_0_.refs_1_.refs_2_.refs_3_, ...), custom_call_target="tpu_custom_call" | custom-call | tf_op jit(solution)/shard_map/pallas_call | solution.py:885
  519.6 7.2 shard_map.355
  526.9 12.7 %shard_map.356 = (bf16[512,1024]{1,0:T(8,128)(2,1)}, bf16[1024,512]{1,0:T(8,128)(2,1)}) custom-call(s32[1]{0:T(128)} %dynamic_slice.44.size_ref, bf16[512,1024]{1,0:T(8,128)(2,1)} %get-tuple-element.183.q_ref, bf16[1024,512]{1,0:T(8,128)(2,1)} %copy-done.14, bf16[512,1024]{1,0:T(8,128)(2,1)} %get-tuple-element.240.do_ref, ...), custom_call_target="tpu_custom_call" | custom-call | tf_op jit(solution)/shard_map/pallas_call | solution.py:366
  539.5 11.9 %convolution_convert_fusion.3 = bf16[2048,1152]{1,0:T(8,128)(2,1)S(1)} fusion(bf16[2048,1792]{1,0:T(8,128)(2,1)} %get-tuple-element.246, bf16[1792,1152]{1,0:T(8,128)(2,1)S(1)} %copy-done.19), kind=kOutput, calls=%fused_computation.10 | convolution fusion | flops 8458076160 | bytes 16187392 | tf_op jit(solution)/shard_map/dot_general | solution.py:23
  551.4 29.5 %collective-permute-done.30.refs_3_ = bf16[4,48,3584]{2,1,0:T(8,128)(2,1)} collective-permute-done((bf16[4,48,3584]{2,1,0:T(8,128)(2,1)}, bf16[4,48,3584]{2,1,0:T(8,128)(2,1)}, u32[]{:S(2)}, u32[]{:S(2)}) %collective-permute-start.30) | collective-permute-done | bytes 1376288 | tf_op jit(solution)/shard_map/ppermute | solution.py:36
  599.2 7.7 shard_map.359
  610.8 12.3 %collective-permute-done.31 = bf16[224,3584]{1,0:T(8,128)(2,1)} collective-permute-done((bf16[224,3584]{1,0:T(8,128)(2,1)}, bf16[224,3584]{1,0:T(8,128)(2,1)}, u32[]{:S(2)}, u32[]{:S(2)}) %collective-permute-start.31) | collective-permute-done | bytes 1605664 | tf_op jit(solution)/shard_map/ppermute | solution.py:36
  642.6 56.9 %collective-permute-done.36.refs_1_ = bf16[224,3584]{1,0:T(8,128)(2,1)S(1)} collective-permute-done((bf16[224,3584]{1,0:T(8,128)(2,1)S(1)}, bf16[224,3584]{1,0:T(8,128)(2,1)S(1)}, u32[]{:S(2)}, u32[]{:S(2)}) %collective-permute-start.36) | collective-permute-done | bytes 1605664 | tf_op jit(solution)/shard_map/ppermute | solution.py:36
  705.3 15.5 %shard_map.363 = bf16[8,896,256]{2,1,0:T(8,128)(2,1)} custom-call(s32[8]{0:T(128)} %iota.55.refs_0_, bf16[544,1536]{1,0:T(8,128)(2,1)} %fusion.8.refs_1_, bf16[544,1536]{1,0:T(8,128)(2,1)} %copy-done.12, bf16[544,1536]{1,0:T(8,128)(2,1)} %copy-done.13, bf16[544,1536]{1,0:T(8,128)(2,1)} %collective-permute-done.39.refs_4_, ...), custom_call_target="tpu_custom_call" | custom-call | tf_op jit(solution)/shard_map/pallas_call | solution.py:192
  721.6 9.8 %shard_map.361 = bf16[8,912,256]{2,1,0:T(8,128)(2,1)} custom-call(s32[8]{0:T(128)} %iota.54.refs_0_, bf16[544,1536]{1,0:T(8,128)(2,1)} %fusion.8.refs_1_, bf16[544,1536]{1,0:T(8,128)(2,1)} %copy-done.12, bf16[544,1536]{1,0:T(8,128)(2,1)} %copy-done.13, bf16[544,1536]{1,0:T(8,128)(2,1)} %collective-permute-done.39.refs_4_, bf16[1152,1536]{1,0:T(8,128)(2,1)} %copy-done.4, ...), custom_call_target="tpu_custom_call" | custom-call | tf_op jit(solution)/shard_map/pallas_call | solution.py:192
  753.0 51.5 %collective-permute-done.42 = bf16[256,1152]{1,0:T(8,128)(2,1)} collective-permute-done((bf16[256,1152]{1,0:T(8,128)(2,1)}, bf16[256,1152]{1,0:T(8,128)(2,1)}, u32[]{:S(2)}, u32[]{:S(2)}) %collective-permute-start.42) | collective-permute-done | bytes 589856 | tf_op jit(solution)/shard_map/ppermute | solution.py:36
  804.5 8.5 collective-permute-done.41
  813.0 25.7 %collective-permute-done.40 = bf16[256,1152]{1,0:T(8,128)(2,1)} collective-permute-done((bf16[256,1152]{1,0:T(8,128)(2,1)}, bf16[256,1152]{1,0:T(8,128)(2,1)}, u32[]{:S(2)}, u32[]{:S(2)}) %collective-permute-start.40) | collective-permute-done | bytes 589856 | tf_op jit(solution)/shard_map/ppermute | solution.py:36
  841.9 5.5 all-to-all-start.4
  865.1 6.1 shard_map.365
  (309 shorter events, 246.4 us)
Async XLA Ops:
  7.2 139.6 %all-gather.3.cloned.1.call-start = ((), (), s32[]{:S(2)}) async-start(), calls=%async_computation.7 | async-start | bytes 6340608 | tf_op jit(solution)/shard_map/all_gather | solution.py:1081
  21.8 65.9 %all-to-all-start = ((bf16[4,128,1152]{2,1,0:T(8,128)(2,1)}), bf16[4,128,1152]{2,1,0:T(8,128)(2,1)S(1)}, u32[]{:S(2)}, u32[]{:S(2)}) async-start(bf16[4,128,1152]{2,1,0:T(8,128)(2,1)} %gather_fusion), calls=%async_computation | async-start | bytes 2359296 | tf_op jit(solution)/shard_map/all_to_all | solution.py:1082
  30.6 55.3 %collective-permute-start.1 = (bf16[128,1152]{1,0:T(8,128)(2,1)S(1)}, bf16[128,1152]{1,0:T(8,128)(2,1)S(1)}, u32[]{:S(2)}, u32[]{:S(2)}) collective-permute-start(bf16[128,1152]{1,0:T(8,128)(2,1)S(1)} %get-tuple-element.331), channel_id=1, source_target_pairs={{0,4},{1,5},{2,6},{3,7},{4,0},{5,1},{6,2},{7,3},{8,12},{9,13},{10,... | collective-permute-start | bytes 884744 | tf_op jit(solution)/shard_map/ppermute | solution.py:36
  30.6 55.3 %collective-permute-start = (bf16[128,1152]{1,0:T(8,128)(2,1)S(1)}, bf16[128,1152]{1,0:T(8,128)(2,1)S(1)}, u32[]{:S(2)}, u32[]{:S(2)}) collective-permute-start(bf16[128,1152]{1,0:T(8,128)(2,1)S(1)} %get-tuple-element.332), channel_id=1, source_target_pairs={{0,2},{1,3},{2,0},{3,1},{4,6},{5,7},{6,4},{7,5},{8,10},{9,11},{10,... | collective-permute-start | bytes 884744 | tf_op jit(solution)/shard_map/ppermute | solution.py:36
  87.7 59.1 %all-to-all-start.1 = ((bf16[4,84,3584]{2,1,0:T(8,128)(2,1)}), bf16[4,84,3584]{2,1,0:T(8,128)(2,1)}, u32[]{:S(2)}, u32[]{:S(2)}) async-start(bf16[4,84,3584]{2,1,0:T(8,128)(2,1)} %shard_map.339), calls=%async_computation.1 | async-start | bytes 5046272 | tf_op jit(solution)/shard_map/all_to_all | solution.py:1022
  92.3 257.4 %all-gather.5.cloned.1.call-start = ((), (), s32[]{:S(2)}) async-start(), calls=%async_computation.8 | async-start | bytes 2064384 | tf_op jit(solution)/shard_map/all_gather | solution.py:1122
  95.7 37.5 %collective-permute-start.4 = (bf16[128,1152]{1,0:T(8,128)(2,1)S(1)}, bf16[128,1152]{1,0:T(8,128)(2,1)S(1)}, u32[]{:S(2)}, u32[]{:S(2)}) collective-permute-start(bf16[128,1152]{1,0:T(8,128)(2,1)S(1)} %get-tuple-element.327), channel_id=1, source_target_pairs={{0,4},{1,5},{2,6},{3,7},{4,0},{5,1},{6,2},{7,3},{8,12},{9,13},{10,... | collective-permute-start | bytes 884744 | tf_op jit(solution)/shard_map/ppermute | solution.py:36
  96.7 49.0 %collective-permute-start.3 = (bf16[128,1152]{1,0:T(8,128)(2,1)S(1)}, bf16[128,1152]{1,0:T(8,128)(2,1)S(1)}, u32[]{:S(2)}, u32[]{:S(2)}) collective-permute-start(bf16[128,1152]{1,0:T(8,128)(2,1)S(1)} %get-tuple-element.328), channel_id=1, source_target_pairs={{0,2},{1,3},{2,0},{3,1},{4,6},{5,7},{6,4},{7,5},{8,10},{9,11},{10,... | collective-permute-start | bytes 884744 | tf_op jit(solution)/shard_map/ppermute | solution.py:36
  150.4 71.9 %collective-permute-start.12 = (bf16[224,3584]{1,0:T(8,128)(2,1)}, bf16[224,3584]{1,0:T(8,128)(2,1)}, u32[]{:S(2)}, u32[]{:S(2)}) collective-permute-start(bf16[224,3584]{1,0:T(8,128)(2,1)} %get-tuple-element.204.refs_0_), channel_id=1, source_target_pairs={{0,4},{1,5},{2,6},{3,7},{4,0},{5,1},{6,2},{7,3},{8,12},{9,13},{10,... | collective-permute-start | bytes 4816904 | tf_op jit(solution)/shard_map/ppermute | solution.py:36
  160.4 38.1 %collective-permute-start.10 = (bf16[272,1536]{1,0:T(8,128)(2,1)S(1)}, bf16[272,1536]{1,0:T(8,128)(2,1)S(1)}, u32[]{:S(2)}, u32[]{:S(2)}) collective-permute-start(bf16[272,1536]{1,0:T(8,128)(2,1)S(1)} %fusion.18.refs_1_), channel_id=1, source_target_pairs={{0,16},{8,24},{16,0},{24,8},{1,17},{9,25},{17,1},{25,9},{2,18},{10... | collective-permute-start | bytes 2506760 | tf_op jit(solution)/shard_map/ppermute | solution.py:36
  226.6 38.1 %collective-permute-start.16 = (bf16[224,3584]{1,0:T(8,128)(2,1)}, bf16[224,3584]{1,0:T(8,128)(2,1)S(1)}, u32[]{:S(2)}, u32[]{:S(2)}) collective-permute-start(bf16[224,3584]{1,0:T(8,128)(2,1)} %collective-permute-done.12.refs_1_), channel_id=1, source_target_pairs={{0,8},{8,0},{16,24},{24,16},{1,9},{9,1},{17,25},{25,17},{2,10},{10... | collective-permute-start | bytes 4816904 | tf_op jit(solution)/shard_map/ppermute | solution.py:36
  228.2 38.3 %collective-permute-start.18 = (bf16[224,3584]{1,0:T(8,128)(2,1)}, bf16[224,3584]{1,0:T(8,128)(2,1)}, u32[]{:S(2)}, u32[]{:S(2)}) collective-permute-start(bf16[224,3584]{1,0:T(8,128)(2,1)} %collective-permute-done.12.refs_1_), channel_id=1, source_target_pairs={{0,16},{8,24},{16,0},{24,8},{1,17},{9,25},{17,1},{25,9},{2,18},{10... | collective-permute-start | bytes 4816904 | tf_op jit(solution)/shard_map/ppermute | solution.py:36
  229.7 69.1 %collective-permute-start.15 = (bf16[224,3584]{1,0:T(8,128)(2,1)}, bf16[224,3584]{1,0:T(8,128)(2,1)}, u32[]{:S(2)}, u32[]{:S(2)}) collective-permute-start(bf16[224,3584]{1,0:T(8,128)(2,1)} %get-tuple-element.204.refs_0_), channel_id=1, source_target_pairs={{0,8},{8,0},{16,24},{24,16},{1,9},{9,1},{17,25},{25,17},{2,10},{10... | collective-permute-start | bytes 4816904 | tf_op jit(solution)/shard_map/ppermute | solution.py:36
  231.0 69.2 %collective-permute-start.17 = (bf16[224,3584]{1,0:T(8,128)(2,1)}, bf16[224,3584]{1,0:T(8,128)(2,1)}, u32[]{:S(2)}, u32[]{:S(2)}) collective-permute-start(bf16[224,3584]{1,0:T(8,128)(2,1)} %get-tuple-element.204.refs_0_), channel_id=1, source_target_pairs={{0,16},{8,24},{16,0},{24,8},{1,17},{9,25},{17,1},{25,9},{2,18},{10... | collective-permute-start | bytes 4816904 | tf_op jit(solution)/shard_map/ppermute | solution.py:36
  232.5 61.7 %collective-permute-start.14 = (bf16[4,48,3584]{2,1,0:T(8,128)(2,1)}, bf16[4,48,3584]{2,1,0:T(8,128)(2,1)}, u32[]{:S(2)}, u32[]{:S(2)}) collective-permute-start(bf16[4,48,3584]{2,1,0:T(8,128)(2,1)} %get-tuple-element.185.refs_1_), channel_id=1, source_target_pairs={{0,4},{1,5},{2,6},{3,7},{4,0},{5,1},{6,2},{7,3},{8,12},{9,13},{10,... | collective-permute-start | bytes 4128776 | tf_op jit(solution)/shard_map/ppermute | solution.py:36
  300.2 43.5 %collective-permute-start.20 = (bf16[224,3584]{1,0:T(8,128)(2,1)}, bf16[224,3584]{1,0:T(8,128)(2,1)}, u32[]{:S(2)}, u32[]{:S(2)}) collective-permute-start(bf16[224,3584]{1,0:T(8,128)(2,1)} %collective-permute-done.15.refs_2_), channel_id=1, source_target_pairs={{0,16},{8,24},{16,0},{24,8},{1,17},{9,25},{17,1},{25,9},{2,18},{10... | collective-permute-start | bytes 4816904 | tf_op jit(solution)/shard_map/ppermute | solution.py:36
  301.6 42.0 %collective-permute-start.21 = (bf16[224,3584]{1,0:T(8,128)(2,1)}, bf16[224,3584]{1,0:T(8,128)(2,1)}, u32[]{:S(2)}, u32[]{:S(2)}) collective-permute-start(bf16[224,3584]{1,0:T(8,128)(2,1)} %collective-permute-done.18.refs_5_), channel_id=1, source_target_pairs={{0,8},{8,0},{16,24},{24,16},{1,9},{9,1},{17,25},{25,17},{2,10},{10... | collective-permute-start | bytes 4816904 | tf_op jit(solution)/shard_map/ppermute | solution.py:36
  302.2 41.5 %collective-permute-start.22 = (bf16[512,1152]{1,0:T(8,128)(2,1)S(1)}, bf16[512,1152]{1,0:T(8,128)(2,1)S(1)}, u32[]{:S(2)}, u32[]{:S(2)}) collective-permute-start(bf16[512,1152]{1,0:T(8,128)(2,1)S(1)} %bitcast.146), channel_id=1, source_target_pairs={{0,2},{1,3},{2,0},{3,1},{4,6},{5,7},{6,4},{7,5},{8,10},{9,11},{10,... | collective-permute-start | bytes 3538952 | tf_op jit(solution)/shard_map/ppermute | solution.py:36
  303.9 571.6 %reduce-scatter.5.cloned.1.call-start = ((), (), s32[]{:S(2)}) async-start(), calls=%async_computation.10 | async-start | bytes 4128768 | tf_op jit(solution)/shard_map/reduce_scatter | solution.py:1289
  451.4 38.8 %collective-permute-start.27 = (bf16[512,1152]{1,0:T(8,128)(2,1)S(1)}, bf16[512,1152]{1,0:T(8,128)(2,1)S(1)}, u32[]{:S(2)}, u32[]{:S(2)}) collective-permute-start(bf16[512,1152]{1,0:T(8,128)(2,1)S(1)} %get-tuple-element.324), channel_id=1, source_target_pairs={{0,2},{1,3},{2,0},{3,1},{4,6},{5,7},{6,4},{7,5},{8,10},{9,11},{10,... | collective-permute-start | bytes 3538952 | tf_op jit(solution)/shard_map/ppermute | solution.py:36
  497.9 83.0 %collective-permute-start.28 = (bf16[2,224,3584]{2,1,0:T(8,128)(2,1)}, bf16[2,224,3584]{2,1,0:T(8,128)(2,1)}, u32[]{:S(2)}, u32[]{:S(2)}) collective-permute-start(bf16[2,224,3584]{2,1,0:T(8,128)(2,1)} %shard_map.352), channel_id=1, source_target_pairs={{0,16},{8,24},{16,0},{24,8},{1,17},{9,25},{17,1},{25,9},{2,18},{10... | collective-permute-start | bytes 9633800 | tf_op jit(solution)/shard_map/ppermute | solution.py:36
  498.4 82.4 %collective-permute-start.29 = (bf16[2,224,3584]{2,1,0:T(8,128)(2,1)}, bf16[2,224,3584]{2,1,0:T(8,128)(2,1)}, u32[]{:S(2)}, u32[]{:S(2)}) collective-permute-start(bf16[2,224,3584]{2,1,0:T(8,128)(2,1)} %shard_map.353), channel_id=1, source_target_pairs={{0,8},{8,0},{16,24},{24,16},{1,9},{9,1},{17,25},{25,17},{2,10},{10... | collective-permute-start | bytes 9633800 | tf_op jit(solution)/shard_map/ppermute | solution.py:36
  519.4 61.5 %collective-permute-start.30 = (bf16[4,48,3584]{2,1,0:T(8,128)(2,1)}, bf16[4,48,3584]{2,1,0:T(8,128)(2,1)}, u32[]{:S(2)}, u32[]{:S(2)}) collective-permute-start(bf16[4,48,3584]{2,1,0:T(8,128)(2,1)} %get-tuple-element.247), channel_id=1, source_target_pairs={{0,4},{1,5},{2,6},{3,7},{4,0},{5,1},{6,2},{7,3},{8,12},{9,13},{10,... | collective-permute-start | bytes 4128776 | tf_op jit(solution)/shard_map/ppermute | solution.py:36
  629.0 70.5 %collective-permute-start.36 = (bf16[224,3584]{1,0:T(8,128)(2,1)S(1)}, bf16[224,3584]{1,0:T(8,128)(2,1)S(1)}, u32[]{:S(2)}, u32[]{:S(2)}) collective-permute-start(bf16[224,3584]{1,0:T(8,128)(2,1)S(1)} %fusion.4), channel_id=1, source_target_pairs={{0,4},{1,5},{2,6},{3,7},{4,0},{5,1},{6,2},{7,3},{8,12},{9,13},{10,... | collective-permute-start | bytes 4816904 | tf_op jit(solution)/shard_map/ppermute | solution.py:36
  629.6 69.9 %collective-permute-start.37 = (bf16[544,1536]{1,0:T(8,128)(2,1)S(1)}, bf16[544,1536]{1,0:T(8,128)(2,1)S(1)}, u32[]{:S(2)}, u32[]{:S(2)}) collective-permute-start(bf16[544,1536]{1,0:T(8,128)(2,1)S(1)} %fusion.9), channel_id=1, source_target_pairs={{0,8},{8,0},{16,24},{24,16},{1,9},{9,1},{17,25},{25,17},{2,10},{10... | collective-permute-start | bytes 5013512 | tf_op jit(solution)/shard_map/ppermute | solution.py:36
  631.2 72.9 %collective-permute-start.38 = (bf16[544,1536]{1,0:T(8,128)(2,1)S(1)}, bf16[544,1536]{1,0:T(8,128)(2,1)S(1)}, u32[]{:S(2)}, u32[]{:S(2)}) collective-permute-start(bf16[544,1536]{1,0:T(8,128)(2,1)S(1)} %fusion.10), channel_id=1, source_target_pairs={{0,16},{8,24},{16,0},{24,8},{1,17},{9,25},{17,1},{25,9},{2,18},{10... | collective-permute-start | bytes 5013512 | tf_op jit(solution)/shard_map/ppermute | solution.py:36
  632.9 71.2 %collective-permute-start.39 = (bf16[544,1536]{1,0:T(8,128)(2,1)S(1)}, bf16[544,1536]{1,0:T(8,128)(2,1)}, u32[]{:S(2)}, u32[]{:S(2)}) collective-permute-start(bf16[544,1536]{1,0:T(8,128)(2,1)S(1)} %fusion.11), channel_id=1, source_target_pairs={{0,24},{8,16},{16,8},{24,0},{1,25},{9,17},{17,9},{25,1},{2,26},{10... | collective-permute-start | bytes 5013512 | tf_op jit(solution)/shard_map/ppermute | solution.py:36
  720.8 156.5 %reduce-scatter.3.cloned.1.call-start = ((), (), s32[]{:S(2)}) async-start(), calls=%async_computation.9 | async-start | bytes 4202496 | tf_op jit(solution)/shard_map/reduce_scatter | solution.py:1289
  738.5 103.3 %all-to-all-start.2 = ((bf16[4,84,3584]{2,1,0:T(8,128)(2,1)}), bf16[4,84,3584]{2,1,0:T(8,128)(2,1)S(1)}, u32[]{:S(2)}, u32[]{:S(2)}) async-start(bf16[4,84,3584]{2,1,0:T(8,128)(2,1)} %get-tuple-element.277), calls=%async_computation.2 | async-start | bytes 5046272 | tf_op jit(solution)/shard_map/all_to_all | solution.py:1022
  745.5 59.1 %collective-permute-start.42 = (bf16[256,1152]{1,0:T(8,128)(2,1)}, bf16[256,1152]{1,0:T(8,128)(2,1)}, u32[]{:S(2)}, u32[]{:S(2)}) collective-permute-start(bf16[256,1152]{1,0:T(8,128)(2,1)} %get-tuple-element.315), channel_id=1, source_target_pairs={{0,6},{1,7},{2,4},{3,5},{4,2},{5,3},{6,0},{7,1},{8,14},{9,15},{10,... | collective-permute-start | bytes 1769480 | tf_op jit(solution)/shard_map/ppermute | solution.py:36
  749.5 63.5 %collective-permute-start.41 = (bf16[256,1152]{1,0:T(8,128)(2,1)}, bf16[256,1152]{1,0:T(8,128)(2,1)}, u32[]{:S(2)}, u32[]{:S(2)}) collective-permute-start(bf16[256,1152]{1,0:T(8,128)(2,1)} %get-tuple-element.316), channel_id=1, source_target_pairs={{0,4},{1,5},{2,6},{3,7},{4,0},{5,1},{6,2},{7,3},{8,12},{9,13},{10,... | collective-permute-start | bytes 1769480 | tf_op jit(solution)/shard_map/ppermute | solution.py:36
  749.5 89.2 %collective-permute-start.40 = (bf16[256,1152]{1,0:T(8,128)(2,1)}, bf16[256,1152]{1,0:T(8,128)(2,1)}, u32[]{:S(2)}, u32[]{:S(2)}) collective-permute-start(bf16[256,1152]{1,0:T(8,128)(2,1)} %get-tuple-element.317), channel_id=1, source_target_pairs={{0,2},{1,3},{2,0},{3,1},{4,6},{5,7},{6,4},{7,5},{8,10},{9,11},{10,... | collective-permute-start | bytes 1769480 | tf_op jit(solution)/shard_map/ppermute | solution.py:36
  (70 other events, 1560.3 us)
Sparse Core Ops, SparseCore 0:
  19.3 84.0 all-gather.2
  304.0 36.3 all-gather.4
  720.9 60.9 reduce-scatter.4
  784.1 81.6 reduce-scatter.2
